TPU v7x, 128 devices: a whole 4x4x4 slice. The times are simulated.
128 devices in a mesh: ctx: 64 (over x, y, z), hd: 2 (over core).
Axes of the slice: x: 4, y: 4, z: 4, core: 2. Of those that a mesh axis runs over, the one named last changes fastest.
Arguments:
- tokens: bfloat16 [65536, 640], P(('ctx', 'hd')), may hold values from -6 to 6
- gain_attn: bfloat16 [640], P(('ctx', 'hd')), may hold values from 0.5 to 1.5
- gain_ffn: bfloat16 [640], P(('ctx', 'hd')), may hold values from 0.5 to 1.5
- w_query: bfloat16 [1024, 640], P(('ctx', 'hd')), may hold values from -0.25 to 0.25
- w_keyval: bfloat16 [512, 640], P(('ctx', 'hd')), may hold values from -0.25 to 0.25
- w_out: bfloat16 [1024, 640], P(('ctx', 'hd')), may hold values from -3 to 3
- w_gate: bfloat16 [2048, 640], P(('ctx', 'hd')), may hold values from -0.25 to 0.25
- w_up: bfloat16 [2048, 640], P(('ctx', 'hd')), may hold values from -0.25 to 0.25
- w_down: bfloat16 [2048, 640], P(('ctx', 'hd')), may hold values from -0.125 to 0.125
- cotangent: bfloat16 [65536, 640], P(('ctx', 'hd')), may hold values from -6 to 6
Outputs:
- output: bfloat16 [65536, 640], P(('ctx', 'hd'))
- grad_tokens: float32 [65536, 640], P(('ctx', 'hd'))
- grad_query: float32 [1024, 640], P(('ctx', 'hd'))
- grad_keyval: float32 [512, 640], P(('ctx', 'hd'))
- grad_out: float32 [1024, 640], P(('ctx', 'hd'))
- grad_gate: float32 [2048, 640], P(('ctx', 'hd'))
- grad_up: float32 [2048, 640], P(('ctx', 'hd'))
- grad_down: float32 [2048, 640], P(('ctx', 'hd'))
- grad_gain_attn: float32 [640], P(('ctx', 'hd'))
- grad_gain_ffn: float32 [640], P(('ctx', 'hd'))
All inputs are finite; a program needn't handle non-finite values.
Results may differ from a plain program's by a relative error of at most 0.015.
Values may be sent and summed in bfloat16 or wider, within the bound.
No kernel may reach another device: no remote copies, remote signals or barrier semaphores. Data moves between devices by JAX's collectives and lax.ppermute only.
A program may use at most 192 MiB of HBM per device.

v0:
```python
import math

import jax
import jax.numpy as jnp
from jax import lax
from jax.experimental import pallas as pl
from jax.experimental.pallas import tpu as pltpu
from jax.sharding import PartitionSpec as P

HEADS = 4
HEAD = 256
WIN = 512
SIDE = 4

EPSILON = 1e-06
MASKED = -1e30
AXES = ("ctx", "hd")
BF = jnp.bfloat16
F32 = jnp.float32

SCALE = 1.0 / math.sqrt(HEAD)
TILE = 128
SPAN = WIN + TILE
MEGA = 1 << 20

ORDER = ((0, 0), (1, 2), (2, 1))


def chip_pairs(axis_of_core, steps):
    pairs = []
    for chip in range(SIDE**3):
        spot = [chip // SIDE**2, chip // SIDE % SIDE, chip % SIDE]
        for core in range(2):
            goal = list(spot)
            axis = axis_of_core[core]
            goal[axis] = (goal[axis] + steps) % SIDE
            target = (goal[0] * SIDE + goal[1]) * SIDE + goal[2]
            pairs.append((chip * 2 + core, target * 2 + core))
    return pairs


def to_sibling(value):
    return lax.ppermute(value, "hd", [(0, 1), (1, 0)])


def gather_stage(value, stage):
    return [value] + [
        lax.ppermute(value, AXES, chip_pairs(ORDER[stage], -steps)) for steps in range(1, SIDE)
    ]


def scatter_stage(pieces, stage):
    return [
        lax.ppermute(pieces[steps], AXES, chip_pairs(ORDER[stage], steps))
        for steps in range(1, SIDE)
    ]


def shifted(value, steps):
    count = lax.axis_size(AXES)
    initial, last = (max(0, -steps), min(count, count - steps))
    return lax.ppermute(value, AXES, [(source, source + steps) for source in range(initial, last)])


def times_rows(left, right):
    return lax.dot_general(left, right, (((1,), (1,)), ((), ())), preferred_element_type=F32)


def times_cols(left, right):
    return lax.dot_general(left, right, (((0,), (0,)), ((), ())), preferred_element_type=F32)


def times_plain(left, right):
    return jnp.dot(left, right, preferred_element_type=F32)


def shape(dims, kind):
    return jax.ShapeDtypeStruct(dims, kind)


def run(kernel, outs, *operands, scratch=(), flops=0, limit=48, in_specs=None, out_specs=None, **more):
    moved = sum(one.size * one.dtype.itemsize for one in operands)
    moved += sum(math.prod(one.shape) * one.dtype.itemsize for one in outs)
    specs = {}
    if in_specs is not None:
        specs["in_specs"] = in_specs
    if out_specs is not None:
        specs["out_specs"] = out_specs
    return pl.pallas_call(
        kernel,
        out_shape=outs,
        scratch_shapes=list(scratch),
        cost_estimate=pl.CostEstimate(flops=flops, bytes_accessed=moved, transcendentals=0),
        compiler_params=pltpu.CompilerParams(vmem_limit_bytes=limit * MEGA),
        **specs,
        **more,
    )(*operands)


def selectors(place):
    core = place % 2
    chip = place // 2
    spot = [chip // SIDE**2, chip // SIDE % SIDE, chip % SIDE]

    def device_of(half, first, last, mid):
        owner = jnp.bitwise_xor(core, half)
        x = (spot[0] + first) % SIDE
        y = (spot[1] + jnp.where(owner == 0, mid, last)) % SIDE
        z = (spot[2] + jnp.where(owner == 0, last, mid)) % SIDE
        return ((x * SIDE + y) * SIDE + z) * 2 + owner

    row = jnp.arange(528, dtype=jnp.int32)
    kind, feature = row // HEAD, row % HEAD
    device = device_of(feature // 128, 0 * row, feature // 32 % 4, feature // 8 % 4)
    goal = kind * HEAD + device % 32 * 8 + feature % 8
    column = jnp.arange(1024, dtype=jnp.int32)
    device = device_of(column // 512, column // 32 % 4, column // 128 % 4, column // 8 % 4)
    part = column % 8
    have = jnp.where(part < 4, device * 4 + part, -1)
    keyval = (goal[:, None] == have[None, :]) & (row[:, None] < 512)
    gains = (row[:, None] >= 512) & (part[None, :] == row[:, None] - 508) & (part[None, :] < 6)
    natural = (goal[:HEAD, None] == row[None, :HEAD]).astype(BF)
    return (keyval | gains).astype(BF), natural


def normalise(values, gain):
    inverse = lax.rsqrt(jnp.mean(values * values, axis=-1, keepdims=True) + EPSILON)
    return (values * inverse * gain).astype(BF)


def normalise_back(values, gain, grad):
    inverse = lax.rsqrt(jnp.mean(values * values, axis=-1, keepdims=True) + EPSILON)
    unit = values * inverse
    gain_grad = jnp.sum(grad * unit, axis=0, keepdims=True)
    scaled = grad * gain
    return inverse * (scaled - unit * jnp.mean(scaled * unit, axis=-1, keepdims=True)), gain_grad


def own_mask():
    row = lax.broadcasted_iota(jnp.int32, (HEADS * TILE, TILE), 0) % TILE
    column = lax.broadcasted_iota(jnp.int32, (HEADS * TILE, TILE), 1)
    return column <= row


def folded(wide, own):
    return jnp.concatenate(
        [jnp.where(own, wide[:, WIN:], wide[:, :TILE]), wide[:, TILE:WIN]], axis=1
    )


def unfolded(narrow, own):
    edge = narrow[:, :TILE]
    none = jnp.zeros_like(edge)
    return jnp.concatenate(
        [jnp.where(own, none, edge), narrow[:, TILE:], jnp.where(own, edge, none)], axis=1
    )


def forward_kernel(
    place_ref, tokens_ref, before_ref, select_ref, a0, a1, a2, a3, b0, b1, b2, b3,
    residual_ref, normed_two_ref, normed_ref, query_ref, keyval_ref, attended_ref, probs_ref,
    weight_query_ref, weight_out_ref, weight_keyval_ref, gains_ref,
):
    count = tokens_ref.shape[0]
    halves = ((a0, a1, a2, a3), (b0, b1, b2, b3))
    for head in range(HEADS):
        for half in range(2):
            for last in range(SIDE):
                here = pl.ds(head * HEAD + half * 128 + last * 32, 32)
                weight_query_ref[here, :] = halves[half][last][0, pl.ds(head * 32, 32), :]
                weight_out_ref[here, :] = halves[half][last][1, pl.ds(head * 32, 32), :]
    mixed = jnp.concatenate([one[2] for half in halves for one in half], axis=0)
    sorted_rows = times_plain(select_ref[...], mixed)
    weight_keyval_ref[...] = sorted_rows[:512].astype(BF)
    gains_ref[...] = sorted_rows[512:520]
    gain_one = sorted_rows[512:513]
    gain_two = sorted_rows[513:514]
    inputs = tokens_ref[...].astype(F32)
    normed = normalise(inputs, gain_one)
    normed_ref[...] = normed
    normed_before = normalise(before_ref[...].astype(F32), gain_one)
    weight_keyval = weight_keyval_ref[...]
    keyval_ref[:WIN, :] = times_rows(normed_before, weight_keyval).astype(BF)
    keyval_ref[WIN:, :] = times_rows(normed, weight_keyval).astype(BF)
    for head in range(HEADS):
        query_ref[head] = times_rows(
            normed, weight_query_ref[pl.ds(head * HEAD, HEAD), :]
        ).astype(BF)
    own = own_mask()
    first_key = jnp.where(place_ref[0] == 0, WIN, 0)

    @pl.loop(0, count // TILE)
    def _(tile):
        start = pl.multiple_of(tile * TILE, TILE)
        queries = query_ref[:, pl.ds(start, TILE), :].reshape(HEADS * TILE, HEAD)
        scores = times_rows(queries, keyval_ref[pl.ds(start, SPAN), :HEAD]) * SCALE
        spot = start + lax.broadcasted_iota(jnp.int32, (1, SPAN), 1)
        scores = folded(jnp.where(spot >= first_key, scores, MASKED), own)
        raised = jnp.exp(scores - jnp.max(scores, axis=1, keepdims=True))
        probs = (raised / jnp.sum(raised, axis=1, keepdims=True)).astype(BF)
        probs_ref[pl.ds(pl.multiple_of(tile * HEADS * TILE, TILE), HEADS * TILE), :] = probs
        mixed = times_plain(unfolded(probs, own), keyval_ref[pl.ds(start, SPAN), HEAD:]).astype(BF)
        for head in range(HEADS):
            attended_ref[pl.ds(start, TILE), pl.ds(head * HEAD, HEAD)] = mixed[
                head * TILE : (head + 1) * TILE
            ]

    residual = inputs + times_plain(attended_ref[...], weight_out_ref[...])
    residual_ref[...] = residual
    normed_two_ref[...] = normalise(residual, gain_two)


GELU_A = math.sqrt(2.0 / math.pi)
GELU_B = 0.044715


def ffn_kernel(
    normed_ref, grad_ref, branch_in_ref, normed_grad_in_ref, w0, w1, w2, w3,
    branch_ref, normed_grad_ref, terms_ref, weight_ref, sems,
):
    step = pl.program_id(0)
    pieces = (w0, w1, w2, w3)

    @pl.when(step == 0)
    def _():
        for k in range(SIDE):
            pltpu.make_async_copy(pieces[k], weight_ref.at[k], sems.at[k]).start()
        branch_ref[...] = branch_in_ref[...]
        normed_grad_ref[...] = normed_grad_in_ref[...]

    pltpu.make_async_copy(w0, weight_ref.at[step], sems.at[step]).wait()
    units = weight_ref[step, 0:4].reshape(512, -1)
    down = weight_ref[step, 4:6].reshape(256, -1)
    normed = normed_ref[...]
    grad = grad_ref[...]
    both = times_rows(normed, units)
    gate, up = both[:, :256], both[:, 256:]
    hidden_grad = times_rows(grad, down)
    square = gate * gate
    bend = jnp.tanh(GELU_A * gate * (1.0 + GELU_B * square))
    half = 0.5 * (1.0 + bend)
    active = gate * half
    slope = half + 0.5 * gate * (1.0 - bend * bend) * (GELU_A + (3.0 * GELU_A * GELU_B) * square)
    hidden = (active * up).astype(BF)
    both_grad = jnp.concatenate(
        [(hidden_grad * up * slope).astype(BF), (hidden_grad * active).astype(BF)], axis=1
    )
    branch_ref[...] += times_plain(hidden, down)
    normed_grad_ref[...] += times_plain(both_grad, units)
    terms_ref[0, 0:4] = times_cols(both_grad, normed).astype(BF).reshape(4, 128, -1)
    terms_ref[0, 4:6] = times_cols(hidden, grad).astype(BF).reshape(2, 128, -1)


def ffn(normed_two, cotangent, branch, normed_grad, pieces):
    rows, width = normed_two.shape
    whole = pl.BlockSpec((rows, width), lambda i: (0, 0))
    return run(
        ffn_kernel,
        (
            shape((rows, width), F32),
            shape((rows, width), F32),
            shape((SIDE, 6, 128, width), BF),
        ),
        normed_two, cotangent, branch, normed_grad, *pieces,
        grid=(SIDE,),
        in_specs=[whole] * 4 + [pl.BlockSpec(memory_space=pl.ANY)] * 4,
        out_specs=(whole, whole, pl.BlockSpec((1, 6, 128, width), lambda i: (i, 0, 0, 0))),
        scratch=[pltpu.VMEM((SIDE, 6, 128, width), BF), pltpu.SemaphoreType.DMA((SIDE,))],
        flops=SIDE * 9 * 2 * rows * width * 256,
    )


def middle_kernel(
    residual_ref, normed_grad_ref, cotangent_ref, branch_ref, gains_ref, weight_out_ref, query_ref, keyval_ref, probs_ref, natural_ref,
    output_ref, residual_grad_ref, low_ref, query_grad_ref, own_ref, sent_ref, gain_ref,
    rows_ref, window_ref,
):
    count = residual_ref.shape[0]
    residual = residual_ref[...]
    output_ref[...] = (residual + branch_ref[...]).astype(BF)
    part, gain_grad = normalise_back(residual, gains_ref[1:2, :], normed_grad_ref[...])
    gain_ref[...] = jnp.broadcast_to(gain_grad, gain_ref.shape)
    residual_grad = cotangent_ref[...].astype(F32) + part
    residual_grad_ref[...] = residual_grad
    low = residual_grad.astype(BF)
    low_ref[...] = low
    for head in range(HEADS):
        rows_ref[head] = times_rows(low, weight_out_ref[pl.ds(head * HEAD, HEAD), :]).astype(BF)
    window_ref[...] = jnp.zeros_like(window_ref)
    own = own_mask()

    @pl.loop(0, count // TILE)
    def _(tile):
        start = pl.multiple_of(tile * TILE, TILE)
        span = pl.ds(start, SPAN)
        queries = query_ref[:, pl.ds(start, TILE), :].reshape(HEADS * TILE, HEAD)
        rows = rows_ref[:, pl.ds(start, TILE), :].reshape(HEADS * TILE, HEAD)
        low_probs = probs_ref[pl.ds(pl.multiple_of(tile * HEADS * TILE, TILE), HEADS * TILE), :]
        probs = low_probs.astype(F32)
        prob_grad = folded(times_rows(rows, keyval_ref[span, HEAD:]), own)
        centre = jnp.sum(probs * prob_grad, axis=1, keepdims=True) / jnp.sum(
            probs, axis=1, keepdims=True
        )
        score_grad = unfolded((probs * (prob_grad - centre)).astype(BF), own)
        mixed = (times_plain(score_grad, keyval_ref[span, :HEAD]) * SCALE).astype(BF)
        for head in range(HEADS):
            query_grad_ref[pl.ds(start, TILE), pl.ds(head * HEAD, HEAD)] = mixed[
                head * TILE : (head + 1) * TILE
            ]
        window_ref[span, :HEAD] += times_cols(score_grad, queries) * SCALE
        window_ref[span, HEAD:] += times_cols(unfolded(low_probs, own), rows)

    own_ref[...] = window_ref[WIN:, :]
    natural = natural_ref[...]
    sent_ref[:, :HEAD] = times_plain(window_ref[:WIN, :HEAD].astype(BF), natural).astype(BF)
    sent_ref[:, HEAD:] = times_plain(window_ref[:WIN, HEAD:].astype(BF), natural).astype(BF)


def weights_kernel(
    normed_ref, low_ref, attended_ref, query_grad_ref, weight_query_ref, normed_grad_ref, query_ref, out_ref
):
    query_grad = query_grad_ref[...]
    normed_grad_ref[...] = times_plain(query_grad, weight_query_ref[...])
    query_ref[...] = times_cols(query_grad, normed_ref[...]).astype(BF)
    out_ref[...] = times_cols(attended_ref[...], low_ref[...]).astype(BF)


def last_kernel(
    tokens_ref, normed_ref, own_ref, came_ref, natural_ref, select_ref, weight_keyval_ref, gains_ref,
    partial_ref, residual_grad_ref, gain_two_ref, query_ref, out_ref,
    input_grad_ref, mine_ref, other_ref,
):
    natural = natural_ref[...]
    keyval = jnp.concatenate(
        [
            own_ref[:, :HEAD] + times_rows(came_ref[:, :HEAD], natural),
            own_ref[:, HEAD:] + times_rows(came_ref[:, HEAD:], natural),
        ],
        axis=1,
    ).astype(BF)
    grad = partial_ref[...] + times_plain(keyval, weight_keyval_ref[...])
    part, gain_grad = normalise_back(tokens_ref[...].astype(F32), gains_ref[0:1, :], grad)
    input_grad_ref[...] = residual_grad_ref[...] + part
    row = lax.broadcasted_iota(jnp.int32, (16, gain_grad.shape[1]), 0)
    gain_rows = jnp.where(
        row == 0, gain_grad, jnp.where(row == 1, gain_two_ref[0:1, :], 0.0)
    ).astype(BF)
    rows = jnp.concatenate([times_cols(keyval, normed_ref[...]).astype(BF), gain_rows], axis=0)
    mixed = times_cols(select_ref[...], rows).astype(BF)
    for half in range(2):
        goal = (mine_ref, other_ref)[half]
        for last in range(SIDE):
            first = (half * SIDE + last) * 128
            goal[last, 2] = mixed[first : first + 128]
            for head in range(HEADS):
                here = pl.ds(head * HEAD + half * 128 + last * 32, 32)
                goal[last, 0, pl.ds(head * 32, 32), :] = query_ref[here, :]
                goal[last, 1, pl.ds(head * 32, 32), :] = out_ref[here, :]


def meet_kernel(mine_ref, came_ref, p0, p1, p2, p3):
    p0[...] = mine_ref[0].astype(F32) + came_ref[0].astype(F32)
    for k, goal in ((1, p1), (2, p2), (3, p3)):
        goal[...] = (mine_ref[k].astype(F32) + came_ref[k].astype(F32)).astype(BF)


def sum_kernel(cut, held_ref, c1, c2, c3, *goals):
    total = held_ref[...]
    for one in (c1, c2, c3):
        total = total + one[...].astype(F32)
    if cut == 0:
        goals[0][...] = total
        return
    groups, rows, width = total.shape
    blocks = total.reshape(groups, rows // (SIDE * 8) if cut == 2 else 1, SIDE, 8, width)
    for k in range(SIDE):
        goals[k][...] = blocks[:, :, k].reshape(groups, rows // SIDE, width).astype(goals[k].dtype)


def scattered(mine, came):
    _, groups, rows, width = mine.shape
    pieces = run(
        meet_kernel, [shape((groups, rows, width), F32 if k == 0 else BF) for k in range(SIDE)], mine, came
    )
    for stage in (2, 1, 0):
        rows = pieces[0].shape[1] // SIDE
        outs = [shape((groups, rows, width), F32 if k == 0 else BF) for k in range(SIDE)]
        if stage == 0:
            outs = [shape(pieces[0].shape, F32)]
        pieces = run(
            lambda *refs, stage=stage: sum_kernel(stage, *refs),
            outs,
            pieces[0],
            *scatter_stage(pieces, stage),
        )
    return pieces[0]


def local(tokens, gain_attn, gain_ffn, w_query, w_keyval, w_out, w_gate, w_up, w_down, cotangent):
    row_count, model_width = tokens.shape
    place = lax.axis_index(AXES)

    width = gain_attn.shape[0]
    lane = jnp.arange(model_width, dtype=jnp.int32)
    mine = lane // width == place
    gain_rows = jnp.where(
        mine[None, :], jnp.stack([jnp.tile(gain_attn, 128), jnp.tile(gain_ffn, 128)]), 0
    ).astype(BF)
    payload = jnp.concatenate(
        [w_query, w_out, w_keyval, jnp.pad(gain_rows, ((0, 2), (0, 0))), w_gate, w_up, w_down]
    ).reshape(9, 8, model_width)
    before = shifted(tokens, 1)
    payload = jnp.stack(gather_stage(payload, 0), axis=1)
    payload = jnp.stack(gather_stage(payload, 1), axis=2)
    attn = gather_stage(payload[:3].reshape(3, 128, model_width), 2)
    attn += [to_sibling(one) for one in attn]
    units = gather_stage(payload[3:].reshape(6, 128, model_width), 2)
    others = [to_sibling(one) for one in units]
    select, natural = selectors(place)

    (
        residual, normed_two, normed, queries, keyvals, attended, probs, weight_query, weight_out, weight_keyval, gains
    ) = run(
        forward_kernel,
        (
            shape((row_count, model_width), F32),
            shape((row_count, model_width), BF),
            shape((row_count, model_width), BF),
            shape((HEADS, row_count, HEAD), BF),
            shape((2 * row_count, 2 * HEAD), BF),
            shape((row_count, HEADS * HEAD), BF),
            shape((HEADS * row_count, WIN), BF),
            shape((HEADS * HEAD, model_width), BF),
            shape((HEADS * HEAD, model_width), BF),
            shape((2 * HEAD, model_width), BF),
            shape((8, model_width), F32),
        ),
        place.reshape(1), tokens, before, select, *attn,
        in_specs=[pl.BlockSpec(memory_space=pltpu.SMEM)] + [pl.BlockSpec(memory_space=pltpu.VMEM)] * 11,
        flops=6 * 10**9,
    )

    nothing = jnp.zeros((row_count, model_width), F32)
    branch, normed_grad, mine = ffn(normed_two, cotangent, nothing, nothing, units)
    branch, normed_grad, other = ffn(normed_two, cotangent, branch, normed_grad, others)
    ffn_grads = scattered(mine, to_sibling(other))

    output, residual_grad, low, query_grad, keyval_own, keyval_sent, gain_two_grad = run(
        middle_kernel,
        (
            shape((row_count, model_width), BF),
            shape((row_count, model_width), F32),
            shape((row_count, model_width), BF),
            shape((row_count, HEADS * HEAD), BF),
            shape((row_count, 2 * HEAD), F32),
            shape((row_count, 2 * HEAD), BF),
            shape((8, model_width), F32),
        ),
        residual, normed_grad, cotangent, branch, gains, weight_out, queries, keyvals, probs, natural,
        scratch=[pltpu.VMEM((HEADS, row_count, HEAD), BF), pltpu.VMEM((2 * row_count, 2 * HEAD), F32)],
        flops=5 * 10**9,
    )
    came = shifted(keyval_sent, -1)
    partial, query_term, out_term = run(
        weights_kernel,
        (
            shape((row_count, model_width), F32),
            shape((HEADS * HEAD, model_width), BF),
            shape((HEADS * HEAD, model_width), BF),
        ),
        normed, low, attended, query_grad, weight_query,
        flops=2 * 10**9,
    )
    input_grad, mine, other = run(
        last_kernel,
        (
            shape((row_count, model_width), F32),
            shape((SIDE, 3, 128, model_width), BF),
            shape((SIDE, 3, 128, model_width), BF),
        ),
        tokens, normed, keyval_own, came, natural, select, weight_keyval, gains,
        partial, residual_grad, gain_two_grad, query_term, out_term,
        flops=2 * 10**9,
    )
    attn_grads = scattered(mine, to_sibling(other))
    gain_shares = lax.dynamic_slice_in_dim(attn_grads[2, 4:6], place * width, width, 1)
    ffn_grads = ffn_grads.reshape(3, 16, model_width)
    return (
        output,
        input_grad,
        attn_grads[0],
        attn_grads[2, :4],
        attn_grads[1],
        ffn_grads[0],
        ffn_grads[1],
        ffn_grads[2],
        gain_shares[0],
        gain_shares[1],
    )


def solution(mesh):
    rows, flat = P(AXES, None), P(AXES)
    return jax.shard_map(
        local,
        mesh=mesh,
        in_specs=(rows, flat, flat, rows, rows, rows, rows, rows, rows, rows),
        out_specs=(rows, rows, rows, rows, rows, rows, rows, rows, flat, flat),
        check_vma=False,
    )
```

profile of v0, /device:TPU:0, one launch (start us, length us, event | category | flops | bytes accessed | tf_op | source)
XLA Modules:
  0.0 240.9 jit_solution(1668886387875807902)
XLA Ops:
  2.5 4.3 %concatenate.3 = bf16[72,640]{1,0:T(8,128)(2,1)S(1)} concatenate(bf16[8,640]{1,0:T(8,128)(2,1)} %param.13, bf16[8,640]{1,0:T(8,128)(2,1)} %param.15, bf16[4,640]{1,0:T(4,128)(2,1)} %param.14, bf16[4,640]{1,0:T(4,128)(2,1)S(1)} %pad.4, bf16[16,640]{1,0:T(8,128)(2,1)} %param.16, bf16[16,640]{1,0:T(8,128)(2,1)} %param.17, bf16[16,640]{1,0:T(8,128)(2,1)} %param.18), dimensions={0} | concatenate | bytes 184320 | tf_op jit(solution)/shard_map/concatenate | solution.py:409
  6.9 2.8 %collective-permute-start.1 = (bf16[9,8,640]{2,1,0:T(8,128)(2,1)S(1)}, bf16[9,8,640]{2,1,0:T(8,128)(2,1)S(1)}, u32[]{:S(2)}, u32[]{:S(2)}) collective-permute-start(bf16[9,8,640]{2,1,0:T(8,128)(2,1)S(1)} %bitcast.57), channel_id=1, source_target_pairs={{0,96},{1,97},{2,98},{3,99},{4,100},{5,101},{6,102},{7,103},{8,104... | collective-permute-start | bytes 276488 | tf_op jit(solution)/shard_map/ppermute | solution.py:48
  11.4 2.2 collective-permute-done.1
  13.6 2.7 %collective-permute-done.2 = bf16[9,8,640]{2,1,0:T(8,128)(2,1)S(1)} collective-permute-done((bf16[9,8,640]{2,1,0:T(8,128)(2,1)S(1)}, bf16[9,8,640]{2,1,0:T(8,128)(2,1)S(1)}, u32[]{:S(2)}, u32[]{:S(2)}) %collective-permute-start.2) | collective-permute-done | bytes 92192 | tf_op jit(solution)/shard_map/ppermute | solution.py:48
  17.4 3.1 %collective-permute-start.4 = (bf16[9,4,8,640]{3,2,1,0:T(8,128)(2,1)S(1)}, bf16[9,4,8,640]{3,2,1,0:T(8,128)(2,1)S(1)}, u32[]{:S(2)}, u32[]{:S(2)}) collective-permute-start(bf16[9,4,8,640]{3,2,1,0:T(8,128)(2,1)S(1)} %get-tuple-element.119), channel_id=1, source_target_pairs={{0,24},{1,7},{2,26},{3,1},{4,28},{5,3},{6,30},{7,5},{8,0},{9,15},{... | collective-permute-start | bytes 1105928 | tf_op jit(solution)/shard_map/ppermute | solution.py:48
  23.4 6.0 %collective-permute-done.4 = bf16[9,4,8,640]{3,2,1,0:T(8,128)(2,1)S(1)} collective-permute-done((bf16[9,4,8,640]{3,2,1,0:T(8,128)(2,1)S(1)}, bf16[9,4,8,640]{3,2,1,0:T(8,128)(2,1)S(1)}, u32[]{:S(2)}, u32[]{:S(2)}) %collective-permute-start.4) | collective-permute-done | bytes 368672 | tf_op jit(solution)/shard_map/ppermute | solution.py:48
  29.6 3.8 %collective-permute-done.6 = bf16[9,4,8,640]{3,2,1,0:T(8,128)(2,1)S(1)} collective-permute-done((bf16[9,4,8,640]{3,2,1,0:T(8,128)(2,1)S(1)}, bf16[9,4,8,640]{3,2,1,0:T(8,128)(2,1)S(1)}, u32[]{:S(2)}, u32[]{:S(2)}) %collective-permute-start.6) | collective-permute-done | bytes 368672 | tf_op jit(solution)/shard_map/ppermute | solution.py:48
  33.5 5.8 %collective-permute-start.7 = (bf16[3,128,640]{2,1,0:T(8,128)(2,1)S(1)}, bf16[3,128,640]{2,1,0:T(8,128)(2,1)S(1)}, u32[]{:S(2)}, u32[]{:S(2)}) collective-permute-start(bf16[3,128,640]{2,1,0:T(8,128)(2,1)S(1)} %bitcast.46), channel_id=1, source_target_pairs={{0,6},{1,25},{2,0},{3,27},{4,2},{5,29},{6,4},{7,31},{8,14},{9,1},{... | collective-permute-start | bytes 1474568 | tf_op jit(solution)/shard_map/ppermute | solution.py:48
  40.3 10.7 %collective-permute-done.7.a1 = bf16[3,128,640]{2,1,0:T(8,128)(2,1)S(1)} collective-permute-done((bf16[3,128,640]{2,1,0:T(8,128)(2,1)S(1)}, bf16[3,128,640]{2,1,0:T(8,128)(2,1)S(1)}, u32[]{:S(2)}, u32[]{:S(2)}) %collective-permute-start.7) | collective-permute-done | bytes 491552 | tf_op jit(solution)/shard_map/ppermute | solution.py:48
  51.1 3.8 %collective-permute-start.14 = (bf16[6,128,640]{2,1,0:T(8,128)(2,1)S(1)}, bf16[6,128,640]{2,1,0:T(8,128)(2,1)S(1)}, u32[]{:S(2)}, u32[]{:S(2)}) collective-permute-start(bf16[6,128,640]{2,1,0:T(8,128)(2,1)S(1)} %bitcast.41), channel_id=1, source_target_pairs={{0,6},{1,25},{2,0},{3,27},{4,2},{5,29},{6,4},{7,31},{8,14},{9,1},{... | collective-permute-start | bytes 2949128 | tf_op jit(solution)/shard_map/ppermute | solution.py:48
  61.8 15.2 %collective-permute-done.14.w1 = bf16[6,128,640]{2,1,0:T(8,128)(2,1)S(1)} collective-permute-done((bf16[6,128,640]{2,1,0:T(8,128)(2,1)S(1)}, bf16[6,128,640]{2,1,0:T(8,128)(2,1)S(1)}, u32[]{:S(2)}, u32[]{:S(2)}) %collective-permute-start.14) | collective-permute-done | bytes 983072 | tf_op jit(solution)/shard_map/ppermute | solution.py:48
  78.0 2.9 %collective-permute-done.16.w3 = bf16[6,128,640]{2,1,0:T(8,128)(2,1)} collective-permute-done((bf16[6,128,640]{2,1,0:T(8,128)(2,1)S(1)}, bf16[6,128,640]{2,1,0:T(8,128)(2,1)}, u32[]{:S(2)}, u32[]{:S(2)}) %collective-permute-start.16) | collective-permute-done | bytes 983072 | tf_op jit(solution)/shard_map/ppermute | solution.py:48
  85.4 13.9 %shard_map.177 = (f32[512,640]{1,0:T(8,128)}, bf16[512,640]{1,0:T(8,128)(2,1)S(1)}, bf16[512,640]{1,0:T(8,128)(2,1)S(1)}, bf16[4,512,256]{2,1,0:T(8,128)(2,1)}, ...) custom-call(s32[1]{0:T(128)} %bitcast.place_ref, ...), custom_call_target="tpu_custom_call" | custom-call | flops 6000000000 | bytes 17485828 | tf_op jit(solution)/shard_map/pallas_call | solution.py:89
  100.6 12.7 %shard_map.178 = (f32[512,640]{1,0:T(8,128)}, f32[512,640]{1,0:T(8,128)}, bf16[4,6,128,640]{3,2,1,0:T(8,128)(2,1)}) custom-call(bf16[512,640]{1,0:T(8,128)(2,1)S(1)} %get-tuple-element.65.normed_ref, bf16[512,640]{1,0:T(8,128)(2,1)S(1)} %copy-done.5, f32[512,640]{1,0:T(8,128)} %broadcast_in_dim.18.branch_in_ref.normed_grad_in_ref, ...), custom_call_target="tpu_custom_call" | custom-call | flops 6039797760 | bytes 14417920 | tf_op jit(solution)/shard_map/pallas_call | solution.py:89
  113.4 13.4 %shard_map.179 = (f32[512,640]{1,0:T(8,128)}, f32[512,640]{1,0:T(8,128)}, bf16[4,6,128,640]{3,2,1,0:T(8,128)(2,1)}) custom-call(bf16[512,640]{1,0:T(8,128)(2,1)S(1)} %get-tuple-element.65.normed_ref, bf16[512,640]{1,0:T(8,128)(2,1)S(1)} %copy-done.5, f32[512,640]{1,0:T(8,128)} %get-tuple-element.66.branch_in_ref, ...), custom_call_target="tpu_custom_call" | custom-call | flops 6039797760 | bytes 14417920 | tf_op jit(solution)/shard_map/pallas_call | solution.py:89
  127.4 11.4 %shard_map.180 = (bf16[512,640]{1,0:T(8,128)(2,1)}, f32[512,640]{1,0:T(8,128)}, bf16[512,640]{1,0:T(8,128)(2,1)S(1)}, bf16[512,1024]{1,0:T(8,128)(2,1)S(1)}, f32...) custom-call(f32[512,640]{1,0:T(8,128)} %get-tuple-element.64.residual_ref, ...), custom_call_target="tpu_custom_call" | custom-call | flops 5000000000 | bytes 15507456 | tf_op jit(solution)/shard_map/pallas_call | solution.py:89
  140.2 5.2 %shard_map.181 = (f32[512,640]{1,0:T(8,128)S(1)}, bf16[1024,640]{1,0:T(8,128)(2,1)S(1)}, bf16[1024,640]{1,0:T(8,128)(2,1)}) custom-call(bf16[512,640]{1,0:T(8,128)(2,1)S(1)} %get-tuple-element.76.normed_ref, bf16[512,640]{1,0:T(8,128)(2,1)S(1)} %get-tuple-element.80.low_ref, bf16[512,1024]{1,0:T(8,128)(2,1)S(1)} %copy-done.14, ...), custom_call_target="tpu_custom_call" | custom-call | flops 2000000000 | bytes 8650752 | tf_op jit(solution)/shard_map/pallas_call | solution.py:89
  146.4 7.0 %shard_map.182 = (f32[512,640]{1,0:T(8,128)}, bf16[4,3,128,640]{3,2,1,0:T(8,128)(2,1)}, bf16[4,3,128,640]{3,2,1,0:T(8,128)(2,1)}) custom-call(bf16[512,640]{1,0:T(8,128)(2,1)S(1)} %copy-done.4, bf16[512,640]{1,0:T(8,128)(2,1)S(1)} %get-tuple-element.76.normed_ref, f32[512,512]{1,0:T(8,128)S(1)} %get-tuple-element.77.own_ref, ...), custom_call_target="tpu_custom_call" | custom-call | flops 2000000000 | bytes 15278080 | tf_op jit(solution)/shard_map/pallas_call | solution.py:89
  153.4 3.3 %collective-permute-start.22 = (bf16[4,3,128,640]{3,2,1,0:T(8,128)(2,1)}, bf16[4,3,128,640]{3,2,1,0:T(8,128)(2,1)S(1)}, u32[]{:S(2)}, u32[]{:S(2)}) collective-permute-start(bf16[4,3,128,640]{3,2,1,0:T(8,128)(2,1)} %get-tuple-element.91), channel_id=1, source_target_pairs={{0,1},{1,0},{2,3},{3,2},{4,5},{5,4},{6,7},{7,6},{8,9},{9,8},{10,11... | collective-permute-start | bytes 5898248 | tf_op jit(solution)/shard_map/ppermute | solution.py:43
  156.7 3.8 %collective-permute-done.22.came_ref = bf16[4,3,128,640]{3,2,1,0:T(8,128)(2,1)S(1)} collective-permute-done((bf16[4,3,128,640]{3,2,1,0:T(8,128)(2,1)}, bf16[4,3,128,640]{3,2,1,0:T(8,128)(2,1)S(1)}, u32[]{:S(2)}, u32[]{:S(2)}) %collective-permute-start.22) | collective-permute-done | bytes 1966112 | tf_op jit(solution)/shard_map/ppermute | solution.py:43
  165.4 7.2 %collective-permute-start.24 = (bf16[3,128,640]{2,1,0:T(8,128)(2,1)S(1)}, bf16[3,128,640]{2,1,0:T(8,128)(2,1)S(1)}, u32[]{:S(2)}, u32[]{:S(2)}) collective-permute-start(bf16[3,128,640]{2,1,0:T(8,128)(2,1)S(1)} %get-tuple-element.94), channel_id=1, source_target_pairs={{0,4},{1,17},{2,6},{3,19},{4,0},{5,21},{6,2},{7,23},{8,12},{9,25},... | collective-permute-start | bytes 1474568 | tf_op jit(solution)/shard_map/ppermute | solution.py:54
  172.6 5.1 %shard_map.187 = (f32[6,128,640]{2,1,0:T(8,128)S(1)}, bf16[6,128,640]{2,1,0:T(8,128)(2,1)}, bf16[6,128,640]{2,1,0:T(8,128)(2,1)}, bf16[6,128,640]{2,1,0:T(8,128)(2,1)}) custom-call(bf16[4,6,128,640]{3,2,1,0:T(8,128)(2,1)} %get-tuple-element.104.mine_ref, bf16[4,6,128,640]{3,2,1,0:T(8,128)(2,1)} %collective-permute-done.32.came_ref), custom_call_target="tpu_custom_call" | custom-call | bytes 12779520 | tf_op jit(solution)/shard_map/pallas_call | solution.py:89
  179.8 2.7 %collective-permute-start.35 = (bf16[6,128,640]{2,1,0:T(8,128)(2,1)}, bf16[6,128,640]{2,1,0:T(8,128)(2,1)}, u32[]{:S(2)}, u32[]{:S(2)}) collective-permute-start(bf16[6,128,640]{2,1,0:T(8,128)(2,1)} %get-tuple-element.109), channel_id=1, source_target_pairs={{0,6},{1,25},{2,0},{3,27},{4,2},{5,29},{6,4},{7,31},{8,14},{9,1},{... | collective-permute-start | bytes 2949128 | tf_op jit(solution)/shard_map/ppermute | solution.py:54
  182.4 2.3 collective-permute-done.24.refs_2_
  185.1 12.4 %collective-permute-start.27 = (bf16[3,32,640]{2,1,0:T(8,128)(2,1)S(1)}, bf16[3,32,640]{2,1,0:T(8,128)(2,1)S(1)}, u32[]{:S(2)}, u32[]{:S(2)}) collective-permute-start(bf16[3,32,640]{2,1,0:T(8,128)(2,1)S(1)} %get-tuple-element.98), channel_id=1, source_target_pairs={{0,16},{1,5},{2,18},{3,7},{4,20},{5,1},{6,22},{7,3},{8,24},{9,13},... | collective-permute-start | bytes 368648 | tf_op jit(solution)/shard_map/ppermute | solution.py:54
  197.5 4.2 %collective-permute-done.26.refs_1_ = bf16[3,32,640]{2,1,0:T(8,128)(2,1)S(1)} collective-permute-done((bf16[3,32,640]{2,1,0:T(8,128)(2,1)S(1)}, bf16[3,32,640]{2,1,0:T(8,128)(2,1)S(1)}, u32[]{:S(2)}, u32[]{:S(2)}) %collective-permute-start.26) | collective-permute-done | bytes 122912 | tf_op jit(solution)/shard_map/ppermute | solution.py:54
  204.4 2.2 collective-permute-done.28.refs_3_
  206.7 2.8 %collective-permute-start.29 = (bf16[3,8,640]{2,1,0:T(8,128)(2,1)S(1)}, bf16[3,8,640]{2,1,0:T(8,128)(2,1)S(1)}, u32[]{:S(2)}, u32[]{:S(2)}) collective-permute-start(bf16[3,8,640]{2,1,0:T(8,128)(2,1)S(1)} %get-tuple-element.101), channel_id=1, source_target_pairs={{0,32},{1,33},{2,34},{3,35},{4,36},{5,37},{6,38},{7,39},{8,40},{9,... | collective-permute-start | bytes 92168 | tf_op jit(solution)/shard_map/ppermute | solution.py:54
  209.4 3.7 %collective-permute-start.30 = (bf16[3,8,640]{2,1,0:T(8,128)(2,1)S(1)}, bf16[3,8,640]{2,1,0:T(8,128)(2,1)S(1)}, u32[]{:S(2)}, u32[]{:S(2)}) collective-permute-start(bf16[3,8,640]{2,1,0:T(8,128)(2,1)S(1)} %get-tuple-element.102), channel_id=1, source_target_pairs={{0,64},{1,65},{2,66},{3,67},{4,68},{5,69},{6,70},{7,71},{8,72},{9,... | collective-permute-start | bytes 92168 | tf_op jit(solution)/shard_map/ppermute | solution.py:54
  220.1 2.9 %collective-permute-start.37 = (bf16[6,32,640]{2,1,0:T(8,128)(2,1)S(1)}, bf16[6,32,640]{2,1,0:T(8,128)(2,1)S(1)}, u32[]{:S(2)}, u32[]{:S(2)}) collective-permute-start(bf16[6,32,640]{2,1,0:T(8,128)(2,1)S(1)} %get-tuple-element.112), channel_id=1, source_target_pairs={{0,16},{1,5},{2,18},{3,7},{4,20},{5,1},{6,22},{7,3},{8,24},{9,13},... | collective-permute-start | bytes 737288 | tf_op jit(solution)/shard_map/ppermute | solution.py:54
  224.0 6.1 %collective-permute-done.36.refs_1_ = bf16[6,32,640]{2,1,0:T(8,128)(2,1)S(1)} collective-permute-done((bf16[6,32,640]{2,1,0:T(8,128)(2,1)S(1)}, bf16[6,32,640]{2,1,0:T(8,128)(2,1)S(1)}, u32[]{:S(2)}, u32[]{:S(2)}) %collective-permute-start.36) | collective-permute-done | bytes 245792 | tf_op jit(solution)/shard_map/ppermute | solution.py:54
  231.8 4.1 %collective-permute-start.40 = (bf16[6,8,640]{2,1,0:T(8,128)(2,1)S(1)}, bf16[6,8,640]{2,1,0:T(8,128)(2,1)S(1)}, u32[]{:S(2)}, u32[]{:S(2)}) collective-permute-start(bf16[6,8,640]{2,1,0:T(8,128)(2,1)S(1)} %get-tuple-element.116), channel_id=1, source_target_pairs={{0,64},{1,65},{2,66},{3,67},{4,68},{5,69},{6,70},{7,71},{8,72},{9,... | collective-permute-start | bytes 184328 | tf_op jit(solution)/shard_map/ppermute | solution.py:54
  (131 shorter events, 50.0 us)
Async XLA Ops:
  17.4 12.1 %collective-permute-start.4 = (bf16[9,4,8,640]{3,2,1,0:T(8,128)(2,1)S(1)}, bf16[9,4,8,640]{3,2,1,0:T(8,128)(2,1)S(1)}, u32[]{:S(2)}, u32[]{:S(2)}) collective-permute-start(bf16[9,4,8,640]{3,2,1,0:T(8,128)(2,1)S(1)} %get-tuple-element.119), channel_id=1, source_target_pairs={{0,24},{1,7},{2,26},{3,1},{4,28},{5,3},{6,30},{7,5},{8,0},{9,15},{... | collective-permute-start | bytes 1105928 | tf_op jit(solution)/shard_map/ppermute | solution.py:48
  20.5 9.1 %collective-permute-start.5 = (bf16[9,4,8,640]{3,2,1,0:T(8,128)(2,1)S(1)}, bf16[9,4,8,640]{3,2,1,0:T(8,128)(2,1)S(1)}, u32[]{:S(2)}, u32[]{:S(2)}) collective-permute-start(bf16[9,4,8,640]{3,2,1,0:T(8,128)(2,1)S(1)} %get-tuple-element.119), channel_id=1, source_target_pairs={{0,16},{1,5},{2,18},{3,7},{4,20},{5,1},{6,22},{7,3},{8,24},{9,13},... | collective-permute-start | bytes 1105928 | tf_op jit(solution)/shard_map/ppermute | solution.py:48
  21.1 12.3 %collective-permute-start.6 = (bf16[9,4,8,640]{3,2,1,0:T(8,128)(2,1)S(1)}, bf16[9,4,8,640]{3,2,1,0:T(8,128)(2,1)S(1)}, u32[]{:S(2)}, u32[]{:S(2)}) collective-permute-start(bf16[9,4,8,640]{3,2,1,0:T(8,128)(2,1)S(1)} %get-tuple-element.119), channel_id=1, source_target_pairs={{0,8},{1,3},{2,10},{3,5},{4,12},{5,7},{6,14},{7,1},{8,16},{9,11},{... | collective-permute-start | bytes 1105928 | tf_op jit(solution)/shard_map/ppermute | solution.py:48
  22.1 29.0 %collective-permute-start = (bf16[512,640]{1,0:T(8,128)(2,1)S(1)}, bf16[512,640]{1,0:T(8,128)(2,1)S(1)}, u32[]{:S(2)}, u32[]{:S(2)}) collective-permute-start(bf16[512,640]{1,0:T(8,128)(2,1)S(1)} %copy-done.3), channel_id=1, source_target_pairs={{0,1},{1,2},{2,3},{3,4},{4,5},{5,6},{6,7},{7,8},{8,9},{9,10},{10,1... | collective-permute-start | bytes 1966088 | tf_op jit(solution)/shard_map/ppermute | solution.py:62
  33.5 17.4 %collective-permute-start.7 = (bf16[3,128,640]{2,1,0:T(8,128)(2,1)S(1)}, bf16[3,128,640]{2,1,0:T(8,128)(2,1)S(1)}, u32[]{:S(2)}, u32[]{:S(2)}) collective-permute-start(bf16[3,128,640]{2,1,0:T(8,128)(2,1)S(1)} %bitcast.46), channel_id=1, source_target_pairs={{0,6},{1,25},{2,0},{3,27},{4,2},{5,29},{6,4},{7,31},{8,14},{9,1},{... | collective-permute-start | bytes 1474568 | tf_op jit(solution)/shard_map/ppermute | solution.py:48
  39.3 15.6 %collective-permute-start.8 = (bf16[3,128,640]{2,1,0:T(8,128)(2,1)S(1)}, bf16[3,128,640]{2,1,0:T(8,128)(2,1)}, u32[]{:S(2)}, u32[]{:S(2)}) collective-permute-start(bf16[3,128,640]{2,1,0:T(8,128)(2,1)S(1)} %bitcast.47), channel_id=1, source_target_pairs={{0,4},{1,17},{2,6},{3,19},{4,0},{5,21},{6,2},{7,23},{8,12},{9,25},... | collective-permute-start | bytes 1474568 | tf_op jit(solution)/shard_map/ppermute | solution.py:48
  39.3 15.6 %collective-permute-start.9 = (bf16[3,128,640]{2,1,0:T(8,128)(2,1)S(1)}, bf16[3,128,640]{2,1,0:T(8,128)(2,1)}, u32[]{:S(2)}, u32[]{:S(2)}) collective-permute-start(bf16[3,128,640]{2,1,0:T(8,128)(2,1)S(1)} %bitcast.48), channel_id=1, source_target_pairs={{0,2},{1,9},{2,4},{3,11},{4,6},{5,13},{6,0},{7,15},{8,10},{9,17},{... | collective-permute-start | bytes 1474568 | tf_op jit(solution)/shard_map/ppermute | solution.py:48
  40.3 15.6 %collective-permute-start.10 = (bf16[3,128,640]{2,1,0:T(8,128)(2,1)S(1)}, bf16[3,128,640]{2,1,0:T(8,128)(2,1)S(1)}, u32[]{:S(2)}, u32[]{:S(2)}) collective-permute-start(bf16[3,128,640]{2,1,0:T(8,128)(2,1)S(1)} %bitcast.49), channel_id=1, source_target_pairs={{0,1},{1,0},{2,3},{3,2},{4,5},{5,4},{6,7},{7,6},{8,9},{9,8},{10,11... | collective-permute-start | bytes 1474568 | tf_op jit(solution)/shard_map/ppermute | solution.py:43
  50.9 7.0 %collective-permute-start.11 = (bf16[3,128,640]{2,1,0:T(8,128)(2,1)S(1)}, bf16[3,128,640]{2,1,0:T(8,128)(2,1)S(1)}, u32[]{:S(2)}, u32[]{:S(2)}) collective-permute-start(bf16[3,128,640]{2,1,0:T(8,128)(2,1)S(1)} %collective-permute-done.7.a1), channel_id=1, source_target_pairs={{0,1},{1,0},{2,3},{3,2},{4,5},{5,4},{6,7},{7,6},{8,9},{9,8},{10,11... | collective-permute-start | bytes 1474568 | tf_op jit(solution)/shard_map/ppermute | solution.py:43
  51.1 25.9 %collective-permute-start.14 = (bf16[6,128,640]{2,1,0:T(8,128)(2,1)S(1)}, bf16[6,128,640]{2,1,0:T(8,128)(2,1)S(1)}, u32[]{:S(2)}, u32[]{:S(2)}) collective-permute-start(bf16[6,128,640]{2,1,0:T(8,128)(2,1)S(1)} %bitcast.41), channel_id=1, source_target_pairs={{0,6},{1,25},{2,0},{3,27},{4,2},{5,29},{6,4},{7,31},{8,14},{9,1},{... | collective-permute-start | bytes 2949128 | tf_op jit(solution)/shard_map/ppermute | solution.py:48
  54.9 23.1 %collective-permute-start.15 = (bf16[6,128,640]{2,1,0:T(8,128)(2,1)S(1)}, bf16[6,128,640]{2,1,0:T(8,128)(2,1)}, u32[]{:S(2)}, u32[]{:S(2)}) collective-permute-start(bf16[6,128,640]{2,1,0:T(8,128)(2,1)S(1)} %bitcast.42), channel_id=1, source_target_pairs={{0,4},{1,17},{2,6},{3,19},{4,0},{5,21},{6,2},{7,23},{8,12},{9,25},... | collective-permute-start | bytes 2949128 | tf_op jit(solution)/shard_map/ppermute | solution.py:48
  54.9 26.0 %collective-permute-start.16 = (bf16[6,128,640]{2,1,0:T(8,128)(2,1)S(1)}, bf16[6,128,640]{2,1,0:T(8,128)(2,1)}, u32[]{:S(2)}, u32[]{:S(2)}) collective-permute-start(bf16[6,128,640]{2,1,0:T(8,128)(2,1)S(1)} %bitcast.43), channel_id=1, source_target_pairs={{0,2},{1,9},{2,4},{3,11},{4,6},{5,13},{6,0},{7,15},{8,10},{9,17},{... | collective-permute-start | bytes 2949128 | tf_op jit(solution)/shard_map/ppermute | solution.py:48
  58.7 22.6 %collective-permute-start.13 = (bf16[3,128,640]{2,1,0:T(8,128)(2,1)}, bf16[3,128,640]{2,1,0:T(8,128)(2,1)}, u32[]{:S(2)}, u32[]{:S(2)}) collective-permute-start(bf16[3,128,640]{2,1,0:T(8,128)(2,1)} %collective-permute-done.9.a3), channel_id=1, source_target_pairs={{0,1},{1,0},{2,3},{3,2},{4,5},{5,4},{6,7},{7,6},{8,9},{9,8},{10,11... | collective-permute-start | bytes 1474568 | tf_op jit(solution)/shard_map/ppermute | solution.py:43
  61.3 52.0 %collective-permute-start.17 = (bf16[6,128,640]{2,1,0:T(8,128)(2,1)S(1)}, bf16[6,128,640]{2,1,0:T(8,128)(2,1)S(1)}, u32[]{:S(2)}, u32[]{:S(2)}) collective-permute-start(bf16[6,128,640]{2,1,0:T(8,128)(2,1)S(1)} %bitcast.44), channel_id=1, source_target_pairs={{0,1},{1,0},{2,3},{3,2},{4,5},{5,4},{6,7},{7,6},{8,9},{9,8},{10,11... | collective-permute-start | bytes 2949128 | tf_op jit(solution)/shard_map/ppermute | solution.py:43
  77.0 36.3 %collective-permute-start.18 = (bf16[6,128,640]{2,1,0:T(8,128)(2,1)S(1)}, bf16[6,128,640]{2,1,0:T(8,128)(2,1)S(1)}, u32[]{:S(2)}, u32[]{:S(2)}) collective-permute-start(bf16[6,128,640]{2,1,0:T(8,128)(2,1)S(1)} %collective-permute-done.14.w1), channel_id=1, source_target_pairs={{0,1},{1,0},{2,3},{3,2},{4,5},{5,4},{6,7},{7,6},{8,9},{9,8},{10,11... | collective-permute-start | bytes 2949128 | tf_op jit(solution)/shard_map/ppermute | solution.py:43
  78.0 35.4 %collective-permute-start.19 = (bf16[6,128,640]{2,1,0:T(8,128)(2,1)}, bf16[6,128,640]{2,1,0:T(8,128)(2,1)S(1)}, u32[]{:S(2)}, u32[]{:S(2)}) collective-permute-start(bf16[6,128,640]{2,1,0:T(8,128)(2,1)} %collective-permute-done.15.w2), channel_id=1, source_target_pairs={{0,1},{1,0},{2,3},{3,2},{4,5},{5,4},{6,7},{7,6},{8,9},{9,8},{10,11... | collective-permute-start | bytes 2949128 | tf_op jit(solution)/shard_map/ppermute | solution.py:43
  80.9 32.5 %collective-permute-start.20 = (bf16[6,128,640]{2,1,0:T(8,128)(2,1)}, bf16[6,128,640]{2,1,0:T(8,128)(2,1)S(1)}, u32[]{:S(2)}, u32[]{:S(2)}) collective-permute-start(bf16[6,128,640]{2,1,0:T(8,128)(2,1)} %collective-permute-done.16.w3), channel_id=1, source_target_pairs={{0,1},{1,0},{2,3},{3,2},{4,5},{5,4},{6,7},{7,6},{8,9},{9,8},{10,11... | collective-permute-start | bytes 2949128 | tf_op jit(solution)/shard_map/ppermute | solution.py:43
  126.8 45.8 %collective-permute-start.32 = (bf16[4,6,128,640]{3,2,1,0:T(8,128)(2,1)}, bf16[4,6,128,640]{3,2,1,0:T(8,128)(2,1)}, u32[]{:S(2)}, u32[]{:S(2)}) collective-permute-start(bf16[4,6,128,640]{3,2,1,0:T(8,128)(2,1)} %get-tuple-element.105), channel_id=1, source_target_pairs={{0,1},{1,0},{2,3},{3,2},{4,5},{5,4},{6,7},{7,6},{8,9},{9,8},{10,11... | collective-permute-start | bytes 11796488 | tf_op jit(solution)/shard_map/ppermute | solution.py:43
  138.9 7.6 %collective-permute-start.21 = (bf16[512,512]{1,0:T(8,128)(2,1)S(1)}, bf16[512,512]{1,0:T(8,128)(2,1)S(1)}, u32[]{:S(2)}, u32[]{:S(2)}) collective-permute-start(bf16[512,512]{1,0:T(8,128)(2,1)S(1)} %get-tuple-element.78), channel_id=1, source_target_pairs={{1,0},{2,1},{3,2},{4,3},{5,4},{6,5},{7,6},{8,7},{9,8},{10,9},{11,1... | collective-permute-start | bytes 1572872 | tf_op jit(solution)/shard_map/ppermute | solution.py:62
  153.4 7.1 %collective-permute-start.22 = (bf16[4,3,128,640]{3,2,1,0:T(8,128)(2,1)}, bf16[4,3,128,640]{3,2,1,0:T(8,128)(2,1)S(1)}, u32[]{:S(2)}, u32[]{:S(2)}) collective-permute-start(bf16[4,3,128,640]{3,2,1,0:T(8,128)(2,1)} %get-tuple-element.91), channel_id=1, source_target_pairs={{0,1},{1,0},{2,3},{3,2},{4,5},{5,4},{6,7},{7,6},{8,9},{9,8},{10,11... | collective-permute-start | bytes 5898248 | tf_op jit(solution)/shard_map/ppermute | solution.py:43
  165.3 14.5 %collective-permute-start.23 = (bf16[3,128,640]{2,1,0:T(8,128)(2,1)S(1)}, bf16[3,128,640]{2,1,0:T(8,128)(2,1)S(1)}, u32[]{:S(2)}, u32[]{:S(2)}) collective-permute-start(bf16[3,128,640]{2,1,0:T(8,128)(2,1)S(1)} %get-tuple-element.93), channel_id=1, source_target_pairs={{0,2},{1,9},{2,4},{3,11},{4,6},{5,13},{6,0},{7,15},{8,10},{9,17},{... | collective-permute-start | bytes 1474568 | tf_op jit(solution)/shard_map/ppermute | solution.py:54
  165.4 19.3 %collective-permute-start.24 = (bf16[3,128,640]{2,1,0:T(8,128)(2,1)S(1)}, bf16[3,128,640]{2,1,0:T(8,128)(2,1)S(1)}, u32[]{:S(2)}, u32[]{:S(2)}) collective-permute-start(bf16[3,128,640]{2,1,0:T(8,128)(2,1)S(1)} %get-tuple-element.94), channel_id=1, source_target_pairs={{0,4},{1,17},{2,6},{3,19},{4,0},{5,21},{6,2},{7,23},{8,12},{9,25},... | collective-permute-start | bytes 1474568 | tf_op jit(solution)/shard_map/ppermute | solution.py:54
  172.6 12.2 %collective-permute-start.25 = (bf16[3,128,640]{2,1,0:T(8,128)(2,1)S(1)}, bf16[3,128,640]{2,1,0:T(8,128)(2,1)S(1)}, u32[]{:S(2)}, u32[]{:S(2)}) collective-permute-start(bf16[3,128,640]{2,1,0:T(8,128)(2,1)S(1)} %get-tuple-element.95), channel_id=1, source_target_pairs={{0,6},{1,25},{2,0},{3,27},{4,2},{5,29},{6,4},{7,31},{8,14},{9,1},{... | collective-permute-start | bytes 1474568 | tf_op jit(solution)/shard_map/ppermute | solution.py:54
  177.7 40.4 %collective-permute-start.33 = (bf16[6,128,640]{2,1,0:T(8,128)(2,1)}, bf16[6,128,640]{2,1,0:T(8,128)(2,1)S(1)}, u32[]{:S(2)}, u32[]{:S(2)}) collective-permute-start(bf16[6,128,640]{2,1,0:T(8,128)(2,1)} %get-tuple-element.107), channel_id=1, source_target_pairs={{0,2},{1,9},{2,4},{3,11},{4,6},{5,13},{6,0},{7,15},{8,10},{9,17},{... | collective-permute-start | bytes 2949128 | tf_op jit(solution)/shard_map/ppermute | solution.py:54
  179.8 38.4 %collective-permute-start.34 = (bf16[6,128,640]{2,1,0:T(8,128)(2,1)}, bf16[6,128,640]{2,1,0:T(8,128)(2,1)}, u32[]{:S(2)}, u32[]{:S(2)}) collective-permute-start(bf16[6,128,640]{2,1,0:T(8,128)(2,1)} %get-tuple-element.108), channel_id=1, source_target_pairs={{0,4},{1,17},{2,6},{3,19},{4,0},{5,21},{6,2},{7,23},{8,12},{9,25},... | collective-permute-start | bytes 2949128 | tf_op jit(solution)/shard_map/ppermute | solution.py:54
  179.8 38.3 %collective-permute-start.35 = (bf16[6,128,640]{2,1,0:T(8,128)(2,1)}, bf16[6,128,640]{2,1,0:T(8,128)(2,1)}, u32[]{:S(2)}, u32[]{:S(2)}) collective-permute-start(bf16[6,128,640]{2,1,0:T(8,128)(2,1)} %get-tuple-element.109), channel_id=1, source_target_pairs={{0,6},{1,25},{2,0},{3,27},{4,2},{5,29},{6,4},{7,31},{8,14},{9,1},{... | collective-permute-start | bytes 2949128 | tf_op jit(solution)/shard_map/ppermute | solution.py:54
  185.0 16.7 %collective-permute-start.26 = (bf16[3,32,640]{2,1,0:T(8,128)(2,1)S(1)}, bf16[3,32,640]{2,1,0:T(8,128)(2,1)S(1)}, u32[]{:S(2)}, u32[]{:S(2)}) collective-permute-start(bf16[3,32,640]{2,1,0:T(8,128)(2,1)S(1)} %get-tuple-element.97), channel_id=1, source_target_pairs={{0,8},{1,3},{2,10},{3,5},{4,12},{5,7},{6,14},{7,1},{8,16},{9,11},{... | collective-permute-start | bytes 368648 | tf_op jit(solution)/shard_map/ppermute | solution.py:54
  185.1 19.3 %collective-permute-start.27 = (bf16[3,32,640]{2,1,0:T(8,128)(2,1)S(1)}, bf16[3,32,640]{2,1,0:T(8,128)(2,1)S(1)}, u32[]{:S(2)}, u32[]{:S(2)}) collective-permute-start(bf16[3,32,640]{2,1,0:T(8,128)(2,1)S(1)} %get-tuple-element.98), channel_id=1, source_target_pairs={{0,16},{1,5},{2,18},{3,7},{4,20},{5,1},{6,22},{7,3},{8,24},{9,13},... | collective-permute-start | bytes 368648 | tf_op jit(solution)/shard_map/ppermute | solution.py:54
  220.0 10.1 %collective-permute-start.36 = (bf16[6,32,640]{2,1,0:T(8,128)(2,1)S(1)}, bf16[6,32,640]{2,1,0:T(8,128)(2,1)S(1)}, u32[]{:S(2)}, u32[]{:S(2)}) collective-permute-start(bf16[6,32,640]{2,1,0:T(8,128)(2,1)S(1)} %get-tuple-element.111), channel_id=1, source_target_pairs={{0,8},{1,3},{2,10},{3,5},{4,12},{5,7},{6,14},{7,1},{8,16},{9,11},{... | collective-permute-start | bytes 737288 | tf_op jit(solution)/shard_map/ppermute | solution.py:54
  220.1 10.0 %collective-permute-start.37 = (bf16[6,32,640]{2,1,0:T(8,128)(2,1)S(1)}, bf16[6,32,640]{2,1,0:T(8,128)(2,1)S(1)}, u32[]{:S(2)}, u32[]{:S(2)}) collective-permute-start(bf16[6,32,640]{2,1,0:T(8,128)(2,1)S(1)} %get-tuple-element.112), channel_id=1, source_target_pairs={{0,16},{1,5},{2,18},{3,7},{4,20},{5,1},{6,22},{7,3},{8,24},{9,13},... | collective-permute-start | bytes 737288 | tf_op jit(solution)/shard_map/ppermute | solution.py:54
  223.0 8.0 %collective-permute-start.38 = (bf16[6,32,640]{2,1,0:T(8,128)(2,1)S(1)}, bf16[6,32,640]{2,1,0:T(8,128)(2,1)S(1)}, u32[]{:S(2)}, u32[]{:S(2)}) collective-permute-start(bf16[6,32,640]{2,1,0:T(8,128)(2,1)S(1)} %get-tuple-element.113), channel_id=1, source_target_pairs={{0,24},{1,7},{2,26},{3,1},{4,28},{5,3},{6,30},{7,5},{8,0},{9,15},{... | collective-permute-start | bytes 737288 | tf_op jit(solution)/shard_map/ppermute | solution.py:54
  231.8 7.0 %collective-permute-start.40 = (bf16[6,8,640]{2,1,0:T(8,128)(2,1)S(1)}, bf16[6,8,640]{2,1,0:T(8,128)(2,1)S(1)}, u32[]{:S(2)}, u32[]{:S(2)}) collective-permute-start(bf16[6,8,640]{2,1,0:T(8,128)(2,1)S(1)} %get-tuple-element.116), channel_id=1, source_target_pairs={{0,64},{1,65},{2,66},{3,67},{4,68},{5,69},{6,70},{7,71},{8,72},{9,... | collective-permute-start | bytes 184328 | tf_op jit(solution)/shard_map/ppermute | solution.py:54
  (29 other events, 153.8 us)
where the time goes:
time: 242 us; the launch traced here: 241 us
  Pallas kernels  73 us (30%)
  waiting for transfers between devices  72.4 us (30%)
  starting transfers between devices  71.8 us (30%)
  local copies, waits for them, and re-layouts  20.4 us (8%)
    pallas_call x14, Pallas kernels, run(): pl.pallas_call(kernel, out_shape=outs, scratch_shapes=list(scratch), cost...  73 us
    ppermute x12, waiting for transfers between devices, gather_stage(): lax.ppermute(value, AXES, chip_pairs(ORDER[stage], -steps))  44.8 us
    ppermute x18, starting transfers between devices, scatter_stage(): lax.ppermute(pieces[steps], AXES, chip_pairs(ORDER[stage], steps))  41.7 us
    ppermute x18, waiting for transfers between devices, scatter_stage(): lax.ppermute(pieces[steps], AXES, chip_pairs(ORDER[stage], steps))  23.8 us
    ppermute x12, starting transfers between devices, gather_stage(): lax.ppermute(value, AXES, chip_pairs(ORDER[stage], -steps))  20.7 us
    unnamed x38, local copies, waits for them, and re-layouts  10.6 us
    ppermute x10, starting transfers between devices, to_sibling(): return lax.ppermute(value, 'hd', [(0, 1), (1, 0)])  6.8 us
  transfers between devices with their start and end apart: 42, of which 21 were waited for; matrix products, arithmetic and copies ran while one was open for 2% of the time, Pallas kernels for 24%

commit v1 on v0

--- a/solution.py
+++ b/solution.py
@@ -78,23 +78,26 @@
     return jax.ShapeDtypeStruct(dims, kind)
 
 
-def run(kernel, outs, *operands, scratch=(), flops=0, limit=48, in_specs=None, out_specs=None, **more):
+WHOLE = pl.BlockSpec(memory_space=pltpu.VMEM)
+ANYWHERE = pl.BlockSpec(memory_space=pl.ANY)
+
+
+def run(kernel, outs, *operands, after=(), flops=0, limit=32, in_specs=None, **more):
     moved = sum(one.size * one.dtype.itemsize for one in operands)
     moved += sum(math.prod(one.shape) * one.dtype.itemsize for one in outs)
-    specs = {}
-    if in_specs is not None:
-        specs["in_specs"] = in_specs
-    if out_specs is not None:
-        specs["out_specs"] = out_specs
+    count = len(operands)
+
+    def body(*refs):
+        kernel(*refs[:count], *refs[count + len(after) :])
+
     return pl.pallas_call(
-        kernel,
+        body,
         out_shape=outs,
-        scratch_shapes=list(scratch),
+        in_specs=list(in_specs or [WHOLE] * count) + [ANYWHERE] * len(after),
         cost_estimate=pl.CostEstimate(flops=flops, bytes_accessed=moved, transcendentals=0),
         compiler_params=pltpu.CompilerParams(vmem_limit_bytes=limit * MEGA),
-        **specs,
         **more,
-    )(*operands)
+    )(*operands, *after)
 
 
 def selectors(place):
@@ -154,6 +157,41 @@
     return jnp.concatenate(
         [jnp.where(own, none, edge), narrow[:, TILE:], jnp.where(own, edge, none)], axis=1
     )
+
+
+def payload_kernel(
+    place_ref, query_ref, out_ref, keyval_ref, gate_ref, up_ref, down_ref, gain_one_ref, gain_two_ref, payload_ref
+):
+    width = gain_one_ref.shape[1]
+    row = lax.broadcasted_iota(jnp.int32, (8, query_ref.shape[1]), 0)
+    lane = lax.broadcasted_iota(jnp.int32, (8, query_ref.shape[1]), 1) - place_ref[0] * width
+    gains = jnp.zeros(row.shape, F32)
+    for k, ref in ((4, gain_one_ref), (5, gain_two_ref)):
+        values = ref[...].astype(F32)
+        for i in range(width):
+            gains = jnp.where((row == k) & (lane == i), values[:, i : i + 1], gains)
+    keyval = jnp.concatenate([keyval_ref[...].astype(F32), gains[4:]], axis=0)
+    payload_ref[0] = query_ref[...]
+    payload_ref[1] = out_ref[...]
+    payload_ref[2] = keyval.astype(BF)
+    for k, ref in ((3, gate_ref), (5, up_ref), (7, down_ref)):
+        payload_ref[k : k + 2] = ref[...].reshape(2, 8, -1)
+
+
+def pack_kernel(r0, r1, r2, r3, goal_ref):
+    groups, rows, width = r0.shape
+    for k, ref in enumerate((r0, r1, r2, r3)):
+        goal_ref[:, k] = ref[...]
+
+
+def pack_two_kernel(r0, r1, r2, r3, attn_ref, units_ref):
+    for k, ref in enumerate((r0, r1, r2, r3)):
+        attn_ref[:, :, k] = ref[:3]
+        units_ref[:, :, k] = ref[3:]
+
+
+def nothing_kernel(*refs):
+    pass
 
 
 def forward_kernel(
@@ -215,9 +253,10 @@
 
 
 def ffn_kernel(
-    normed_ref, grad_ref, branch_in_ref, normed_grad_in_ref, w0, w1, w2, w3,
-    branch_ref, normed_grad_ref, terms_ref, weight_ref, sems,
+    first, normed_ref, grad_ref, branch_in_ref, normed_grad_in_ref, w0, w1, w2, w3,
+    branch_ref, normed_grad_ref, terms_ref, *more,
 ):
+    output_ref, (weight_ref, sems) = (None, more) if first else (more[0], more[1:])
     step = pl.program_id(0)
     pieces = (w0, w1, w2, w3)
 
@@ -226,7 +265,7 @@
         for k in range(SIDE):
             pltpu.make_async_copy(pieces[k], weight_ref.at[k], sems.at[k]).start()
         branch_ref[...] = branch_in_ref[...]
-        normed_grad_ref[...] = normed_grad_in_ref[...]
+        normed_grad_ref[...] = jnp.zeros_like(normed_grad_ref) if first else normed_grad_in_ref[...]
 
     pltpu.make_async_copy(w0, weight_ref.at[step], sems.at[step]).wait()
     units = weight_ref[step, 0:4].reshape(512, -1)
@@ -249,35 +288,36 @@
     normed_grad_ref[...] += times_plain(both_grad, units)
     terms_ref[0, 0:4] = times_cols(both_grad, normed).astype(BF).reshape(4, 128, -1)
     terms_ref[0, 4:6] = times_cols(hidden, grad).astype(BF).reshape(2, 128, -1)
-
-
-def ffn(normed_two, cotangent, branch, normed_grad, pieces):
+    if not first:
+
+        @pl.when(step == SIDE - 1)
+        def _():
+            output_ref[...] = branch_ref[...].astype(BF)
+
+
+def ffn(first, normed_two, cotangent, branch, normed_grad, pieces):
     rows, width = normed_two.shape
     whole = pl.BlockSpec((rows, width), lambda i: (0, 0))
+    more = () if first else (shape((rows, width), BF),)
     return run(
-        ffn_kernel,
-        (
-            shape((rows, width), F32),
-            shape((rows, width), F32),
-            shape((SIDE, 6, 128, width), BF),
-        ),
+        lambda *refs: ffn_kernel(first, *refs),
+        (shape((rows, width), F32), shape((rows, width), F32), shape((SIDE, 6, 128, width), BF)) + more,
         normed_two, cotangent, branch, normed_grad, *pieces,
         grid=(SIDE,),
-        in_specs=[whole] * 4 + [pl.BlockSpec(memory_space=pl.ANY)] * 4,
-        out_specs=(whole, whole, pl.BlockSpec((1, 6, 128, width), lambda i: (i, 0, 0, 0))),
-        scratch=[pltpu.VMEM((SIDE, 6, 128, width), BF), pltpu.SemaphoreType.DMA((SIDE,))],
+        in_specs=[whole] * 3 + [ANYWHERE if first else whole] + [ANYWHERE] * 4,
+        out_specs=(whole, whole, pl.BlockSpec((1, 6, 128, width), lambda i: (i, 0, 0, 0))) + (whole,) * len(more),
+        scratch_shapes=[pltpu.VMEM((SIDE, 6, 128, width), BF), pltpu.SemaphoreType.DMA((SIDE,))],
         flops=SIDE * 9 * 2 * rows * width * 256,
     )
 
 
 def middle_kernel(
-    residual_ref, normed_grad_ref, cotangent_ref, branch_ref, gains_ref, weight_out_ref, query_ref, keyval_ref, probs_ref, natural_ref,
-    output_ref, residual_grad_ref, low_ref, query_grad_ref, own_ref, sent_ref, gain_ref,
+    residual_ref, normed_grad_ref, cotangent_ref, gains_ref, weight_out_ref, query_ref, keyval_ref, probs_ref, natural_ref,
+    residual_grad_ref, low_ref, query_grad_ref, own_ref, sent_ref, gain_ref,
     rows_ref, window_ref,
 ):
     count = residual_ref.shape[0]
     residual = residual_ref[...]
-    output_ref[...] = (residual + branch_ref[...]).astype(BF)
     part, gain_grad = normalise_back(residual, gains_ref[1:2, :], normed_grad_ref[...])
     gain_ref[...] = jnp.broadcast_to(gain_grad, gain_ref.shape)
     residual_grad = cotangent_ref[...].astype(F32) + part
@@ -364,58 +404,94 @@
         goal[...] = (mine_ref[k].astype(F32) + came_ref[k].astype(F32)).astype(BF)
 
 
-def sum_kernel(cut, held_ref, c1, c2, c3, *goals):
-    total = held_ref[...]
-    for one in (c1, c2, c3):
+def meet(mine, came, after=()):
+    _, groups, rows, width = mine.shape
+    both = pl.BlockSpec((SIDE, 3, rows, width), lambda i: (0, i, 0, 0))
+    return run(
+        meet_kernel,
+        [shape((groups, rows, width), F32 if k == 0 else BF) for k in range(SIDE)],
+        mine, came,
+        after=after,
+        grid=(groups // 3,),
+        in_specs=[both] * 2,
+        out_specs=[pl.BlockSpec((3, rows, width), lambda i: (i, 0, 0))] * SIDE,
+    )
+
+
+def summed(refs):
+    total = refs[0][...]
+    for one in refs[1:]:
         total = total + one[...].astype(F32)
-    if cut == 0:
-        goals[0][...] = total
-        return
+    return total
+
+
+def middle_sum_kernel(*refs):
+    total = summed(refs[:SIDE])
     groups, rows, width = total.shape
-    blocks = total.reshape(groups, rows // (SIDE * 8) if cut == 2 else 1, SIDE, 8, width)
-    for k in range(SIDE):
-        goals[k][...] = blocks[:, :, k].reshape(groups, rows // SIDE, width).astype(goals[k].dtype)
-
-
-def scattered(mine, came):
-    _, groups, rows, width = mine.shape
-    pieces = run(
-        meet_kernel, [shape((groups, rows, width), F32 if k == 0 else BF) for k in range(SIDE)], mine, came
-    )
-    for stage in (2, 1, 0):
-        rows = pieces[0].shape[1] // SIDE
-        outs = [shape((groups, rows, width), F32 if k == 0 else BF) for k in range(SIDE)]
-        if stage == 0:
-            outs = [shape(pieces[0].shape, F32)]
-        pieces = run(
-            lambda *refs, stage=stage: sum_kernel(stage, *refs),
-            outs,
-            pieces[0],
-            *scatter_stage(pieces, stage),
-        )
-    return pieces[0]
+    blocks = total.reshape(groups, SIDE, SIDE, 8, width)
+    for k, goal in enumerate(refs[SIDE:]):
+        goal[...] = blocks[:, :, k].reshape(groups, 4 * 8, width).astype(goal.dtype)
+
+
+def middle_sum(held, came, after=()):
+    groups, rows, width = held.shape
+    return run(
+        middle_sum_kernel,
+        [shape((groups, rows // SIDE, width), F32 if k == 0 else BF) for k in range(SIDE)],
+        held, *came,
+        after=after,
+        grid=(groups // 3,),
+        in_specs=[pl.BlockSpec((3, rows, width), lambda i: (i, 0, 0))] * SIDE,
+        out_specs=[pl.BlockSpec((3, rows // SIDE, width), lambda i: (i, 0, 0))] * SIDE,
+    )
+
+
+def first_sum_kernel(*refs):
+    for first, groups, parts in ((0, 3, refs[:SIDE]), (3, 6, refs[SIDE : 2 * SIDE])):
+        total = summed(parts)
+        for k, goal in enumerate(refs[2 * SIDE :]):
+            goal[first : first + groups] = total[:, 8 * k : 8 * k + 8].astype(goal.dtype)
+
+
+def end_kernel(place_ref, r0, r1, r2, r3, query_ref, keyval_ref, out_ref, gate_ref, up_ref, down_ref, one_ref, two_ref):
+    total = summed((r0, r1, r2, r3))
+    query_ref[...] = total[0]
+    out_ref[...] = total[1]
+    keyval_ref[...] = total[2, :4]
+    for k, goal in ((3, gate_ref), (5, up_ref), (7, down_ref)):
+        goal[...] = total[k : k + 2].reshape(goal.shape)
+    width = one_ref.shape[0]
+    full = total.shape[-1]
+    rows = pltpu.roll(total[2], lax.rem(full - place_ref[0] * width, full), 1)
+    one_ref[...] = rows[4, :width]
+    two_ref[...] = rows[5, :width]
 
 
 def local(tokens, gain_attn, gain_ffn, w_query, w_keyval, w_out, w_gate, w_up, w_down, cotangent):
     row_count, model_width = tokens.shape
     place = lax.axis_index(AXES)
 
-    width = gain_attn.shape[0]
-    lane = jnp.arange(model_width, dtype=jnp.int32)
-    mine = lane // width == place
-    gain_rows = jnp.where(
-        mine[None, :], jnp.stack([jnp.tile(gain_attn, 128), jnp.tile(gain_ffn, 128)]), 0
-    ).astype(BF)
-    payload = jnp.concatenate(
-        [w_query, w_out, w_keyval, jnp.pad(gain_rows, ((0, 2), (0, 0))), w_gate, w_up, w_down]
-    ).reshape(9, 8, model_width)
     before = shifted(tokens, 1)
-    payload = jnp.stack(gather_stage(payload, 0), axis=1)
-    payload = jnp.stack(gather_stage(payload, 1), axis=2)
-    attn = gather_stage(payload[:3].reshape(3, 128, model_width), 2)
+    spot = place.reshape(1)
+    scalar = pl.BlockSpec(memory_space=pltpu.SMEM)
+    payload, = run(
+        payload_kernel,
+        [shape((9, 8, model_width), BF)],
+        spot, w_query, w_out, w_keyval, w_gate, w_up, w_down, gain_attn[None], gain_ffn[None],
+        in_specs=[scalar] + [WHOLE] * 8,
+    )
+    payload, = run(
+        pack_kernel, [shape((9, SIDE, 8, model_width), BF)], *gather_stage(payload, 0)
+    )
+    attn, units = run(
+        pack_two_kernel,
+        [shape((3, SIDE, SIDE, 8, model_width), BF), shape((6, SIDE, SIDE, 8, model_width), BF)],
+        *gather_stage(payload, 1),
+        after=(before,),
+    )
+    attn = gather_stage(attn.reshape(3, 128, model_width), 2)
+    units = gather_stage(units.reshape(6, 128, model_width), 2)
     attn += [to_sibling(one) for one in attn]
-    units = gather_stage(payload[3:].reshape(6, 128, model_width), 2)
-    others = [to_sibling(one) for one in units]
     select, natural = selectors(place)
 
     (
@@ -435,20 +511,28 @@
             shape((2 * HEAD, model_width), BF),
             shape((8, model_width), F32),
         ),
-        place.reshape(1), tokens, before, select, *attn,
-        in_specs=[pl.BlockSpec(memory_space=pltpu.SMEM)] + [pl.BlockSpec(memory_space=pltpu.VMEM)] * 11,
+        spot, tokens, before, select, *attn,
+        in_specs=[scalar] + [WHOLE] * 11,
         flops=6 * 10**9,
     )
 
-    nothing = jnp.zeros((row_count, model_width), F32)
-    branch, normed_grad, mine = ffn(normed_two, cotangent, nothing, nothing, units)
-    branch, normed_grad, other = ffn(normed_two, cotangent, branch, normed_grad, others)
-    ffn_grads = scattered(mine, to_sibling(other))
-
-    output, residual_grad, low, query_grad, keyval_own, keyval_sent, gain_two_grad = run(
+    units = run(
+        nothing_kernel,
+        [shape(one.shape, one.dtype) for one in units],
+        *units,
+        after=(normed_two,),
+        in_specs=[ANYWHERE] * SIDE,
+        out_specs=[ANYWHERE] * SIDE,
+        input_output_aliases={k: k for k in range(SIDE)},
+    )
+    others = [to_sibling(one) for one in units]
+    branch, normed_grad, mine = ffn(True, normed_two, cotangent, residual, residual, units)
+    branch, normed_grad, other, output = ffn(False, normed_two, cotangent, branch, normed_grad, others)
+    ffn_came = to_sibling(other)
+
+    residual_grad, low, query_grad, keyval_own, keyval_sent, gain_two_grad = run(
         middle_kernel,
         (
-            shape((row_count, model_width), BF),
             shape((row_count, model_width), F32),
             shape((row_count, model_width), BF),
             shape((row_count, HEADS * HEAD), BF),
@@ -456,10 +540,12 @@
             shape((row_count, 2 * HEAD), BF),
             shape((8, model_width), F32),
         ),
-        residual, normed_grad, cotangent, branch, gains, weight_out, queries, keyvals, probs, natural,
-        scratch=[pltpu.VMEM((HEADS, row_count, HEAD), BF), pltpu.VMEM((2 * row_count, 2 * HEAD), F32)],
+        residual, normed_grad, cotangent, gains, weight_out, queries, keyvals, probs, natural,
+        scratch_shapes=[pltpu.VMEM((HEADS, row_count, HEAD), BF), pltpu.VMEM((2 * row_count, 2 * HEAD), F32)],
         flops=5 * 10**9,
     )
+    ffn_pieces = meet(mine, ffn_came, after=(low,))
+    ffn_back = scatter_stage(ffn_pieces, 2)
     came = shifted(keyval_sent, -1)
     partial, query_term, out_term = run(
         weights_kernel,
@@ -469,6 +555,7 @@
             shape((HEADS * HEAD, model_width), BF),
         ),
         normed, low, attended, query_grad, weight_query,
+        after=(ffn_pieces[1],),
         flops=2 * 10**9,
     )
     input_grad, mine, other = run(
@@ -482,21 +569,24 @@
         partial, residual_grad, gain_two_grad, query_term, out_term,
         flops=2 * 10**9,
     )
-    attn_grads = scattered(mine, to_sibling(other))
-    gain_shares = lax.dynamic_slice_in_dim(attn_grads[2, 4:6], place * width, width, 1)
-    ffn_grads = ffn_grads.reshape(3, 16, model_width)
-    return (
-        output,
-        input_grad,
-        attn_grads[0],
-        attn_grads[2, :4],
-        attn_grads[1],
-        ffn_grads[0],
-        ffn_grads[1],
-        ffn_grads[2],
-        gain_shares[0],
-        gain_shares[1],
-    )
+    attn_pieces = meet(mine, to_sibling(other))
+    attn_back = scatter_stage(attn_pieces, 2)
+    ffn_pieces = middle_sum(ffn_pieces[0], ffn_back, after=(attn_pieces[1],))
+    ffn_back = scatter_stage(ffn_pieces, 1)
+    attn_pieces = middle_sum(attn_pieces[0], attn_back, after=(ffn_pieces[1],))
+    attn_back = scatter_stage(attn_pieces, 1)
+    pieces = run(
+        first_sum_kernel,
+        [shape((9, 8, model_width), F32 if k == 0 else BF) for k in range(SIDE)],
+        attn_pieces[0], *attn_back, ffn_pieces[0], *ffn_back,
+    )
+    query, keyval, out, gate, up, down, gain_one, gain_two = run(
+        end_kernel,
+        [shape(one.shape, F32) for one in (w_query, w_keyval, w_out, w_gate, w_up, w_down, gain_attn, gain_ffn)],
+        spot, pieces[0], *scatter_stage(pieces, 0),
+        in_specs=[scalar] + [WHOLE] * SIDE,
+    )
+    return output, input_grad, query, keyval, out, gate, up, down, gain_one, gain_two
 
 
 def solution(mesh):

time: 242 us -> 191 us (0.79)
  Pallas kernels: 73 us -> 51.3 us
  starting transfers between devices: 71.8 us -> 52.3 us
  local copies, waits for them, and re-layouts: 20.4 us -> 15.5 us
  waiting for transfers between devices: 72.4 us -> 68.8 us
    pallas_call x14 -> x16, Pallas kernels: 73 us -> 51.3 us  [run(): pl.pallas_call(body, out_shape=outs, in_specs=list(in_specs or [WHOLE] *...]
    ppermute x18 -> x15, starting transfers between devices: 41.7 us -> 23.8 us  [scatter_stage(): lax.ppermute(pieces[steps], AXES, chip_pairs(ORDER[stage], steps))]
    ppermute x18 -> x15, waiting for transfers between devices: 23.8 us -> 34.6 us  [scatter_stage(): lax.ppermute(pieces[steps], AXES, chip_pairs(ORDER[stage], steps))]
    ppermute x12, waiting for transfers between devices: 44.8 us -> 34.2 us  [gather_stage(): lax.ppermute(value, AXES, chip_pairs(ORDER[stage], -steps))]
    unnamed x38 -> x58, local copies, waits for them, and re-layouts: 10.6 us -> 15.5 us
    concatenate x1 -> x0, local copies, waits for them, and re-layouts: 4.34 us -> none  [local(): jnp.concatenate([w_query, w_out, w_keyval, jnp.pad(gain_rows, ((0, 2), (0...]
    ppermute x10, waiting for transfers between devices: 3.83 us -> 0.03 us  [to_sibling(): return lax.ppermute(value, 'hd', [(0, 1), (1, 0)])]
  transfers between devices with their start and end apart: 42 -> 39, of which waited for: 21 -> 18; matrix products, arithmetic and copies ran while one was open for 2% -> 1% of each run, Pallas kernels for 24% -> 19%
where the time goes in v1:
time: 191 us; the launch traced here: 190 us
  waiting for transfers between devices  68.8 us (36%)
  starting transfers between devices  52.3 us (27%)
  Pallas kernels  51.3 us (27%)
  local copies, waits for them, and re-layouts  15.5 us (8%)
    pallas_call x16, Pallas kernels, run(): pl.pallas_call(body, out_shape=outs, in_specs=list(in_specs or [WHOLE] *...  51.3 us
    ppermute x15, waiting for transfers between devices, scatter_stage(): lax.ppermute(pieces[steps], AXES, chip_pairs(ORDER[stage], steps))  34.6 us
    ppermute x12, waiting for transfers between devices, gather_stage(): lax.ppermute(value, AXES, chip_pairs(ORDER[stage], -steps))  34.2 us
    ppermute x15, starting transfers between devices, scatter_stage(): lax.ppermute(pieces[steps], AXES, chip_pairs(ORDER[stage], steps))  23.8 us
    ppermute x12, starting transfers between devices, gather_stage(): lax.ppermute(value, AXES, chip_pairs(ORDER[stage], -steps))  18.6 us
    unnamed x58, local copies, waits for them, and re-layouts  15.5 us
    ppermute x10, starting transfers between devices, to_sibling(): return lax.ppermute(value, 'hd', [(0, 1), (1, 0)])  6.98 us
  transfers between devices with their start and end apart: 39, of which 18 were waited for; matrix products, arithmetic and copies ran while one was open for 1% of the time, Pallas kernels for 19%

profile of v1, /device:TPU:0, one launch (start us, length us, event | category | flops | bytes accessed | tf_op | source)
XLA Modules:
  0.0 190.0 jit_solution(76063322360089873)
XLA Ops:
  7.7 3.5 %collective-permute-start.1 = (bf16[9,8,640]{2,1,0:T(8,128)(2,1)S(1)}, bf16[9,8,640]{2,1,0:T(8,128)(2,1)S(1)}, u32[]{:S(2)}, u32[]{:S(2)}) collective-permute-start(bf16[9,8,640]{2,1,0:T(8,128)(2,1)S(1)} %shard_map.177.refs_0_), channel_id=1, source_target_pairs={{0,96},{1,97},{2,98},{3,99},{4,100},{5,101},{6,102},{7,103},{8,104... | collective-permute-start | bytes 276488 | tf_op jit(solution)/shard_map/ppermute | solution.py:48
  13.4 4.2 %collective-permute-done.2.refs_2_ = bf16[9,8,640]{2,1,0:T(8,128)(2,1)S(1)} collective-permute-done((bf16[9,8,640]{2,1,0:T(8,128)(2,1)S(1)}, bf16[9,8,640]{2,1,0:T(8,128)(2,1)S(1)}, u32[]{:S(2)}, u32[]{:S(2)}) %collective-permute-start.2) | collective-permute-done | bytes 92192 | tf_op jit(solution)/shard_map/ppermute | solution.py:48
  17.6 2.6 %collective-permute-done.3.refs_3_ = bf16[9,8,640]{2,1,0:T(8,128)(2,1)S(1)} collective-permute-done((bf16[9,8,640]{2,1,0:T(8,128)(2,1)S(1)}, bf16[9,8,640]{2,1,0:T(8,128)(2,1)S(1)}, u32[]{:S(2)}, u32[]{:S(2)}) %collective-permute-start.3) | collective-permute-done | bytes 92192 | tf_op jit(solution)/shard_map/ppermute | solution.py:48
  20.2 3.1 %collective-permute-start.4 = (bf16[9,4,8,640]{3,2,1,0:T(8,128)(2,1)S(1)}, bf16[9,4,8,640]{3,2,1,0:T(8,128)(2,1)S(1)}, u32[]{:S(2)}, u32[]{:S(2)}) collective-permute-start(bf16[9,4,8,640]{3,2,1,0:T(8,128)(2,1)S(1)} %shard_map.178.refs_0_), channel_id=1, source_target_pairs={{0,24},{1,7},{2,26},{3,1},{4,28},{5,3},{6,30},{7,5},{8,0},{9,15},{... | collective-permute-start | bytes 1105928 | tf_op jit(solution)/shard_map/ppermute | solution.py:48
  24.9 7.4 %collective-permute-done.4.refs_1_ = bf16[9,4,8,640]{3,2,1,0:T(8,128)(2,1)S(1)} collective-permute-done((bf16[9,4,8,640]{3,2,1,0:T(8,128)(2,1)S(1)}, bf16[9,4,8,640]{3,2,1,0:T(8,128)(2,1)S(1)}, u32[]{:S(2)}, u32[]{:S(2)}) %collective-permute-start.4) | collective-permute-done | bytes 368672 | tf_op jit(solution)/shard_map/ppermute | solution.py:48
  32.4 3.8 %collective-permute-done.6.refs_3_ = bf16[9,4,8,640]{3,2,1,0:T(8,128)(2,1)S(1)} collective-permute-done((bf16[9,4,8,640]{3,2,1,0:T(8,128)(2,1)S(1)}, bf16[9,4,8,640]{3,2,1,0:T(8,128)(2,1)S(1)}, u32[]{:S(2)}, u32[]{:S(2)}) %collective-permute-start.6) | collective-permute-done | bytes 368672 | tf_op jit(solution)/shard_map/ppermute | solution.py:48
  36.4 2.2 %collective-permute-start.7 = (bf16[3,128,640]{2,1,0:T(8,128)(2,1)S(1)}, bf16[3,128,640]{2,1,0:T(8,128)(2,1)}, u32[]{:S(2)}, u32[]{:S(2)}) collective-permute-start(bf16[3,128,640]{2,1,0:T(8,128)(2,1)S(1)} %bitcast.11), channel_id=1, source_target_pairs={{0,6},{1,25},{2,0},{3,27},{4,2},{5,29},{6,4},{7,31},{8,14},{9,1},{... | collective-permute-start | bytes 1474568 | tf_op jit(solution)/shard_map/ppermute | solution.py:48
  38.6 1.9 collective-permute-start.8
  41.8 8.4 %collective-permute-done.7.refs_5_ = bf16[3,128,640]{2,1,0:T(8,128)(2,1)} collective-permute-done((bf16[3,128,640]{2,1,0:T(8,128)(2,1)S(1)}, bf16[3,128,640]{2,1,0:T(8,128)(2,1)}, u32[]{:S(2)}, u32[]{:S(2)}) %collective-permute-start.7) | collective-permute-done | bytes 491552 | tf_op jit(solution)/shard_map/ppermute | solution.py:48
  50.8 3.4 %collective-permute-done.9.refs_7_ = bf16[3,128,640]{2,1,0:T(8,128)(2,1)} collective-permute-done((bf16[3,128,640]{2,1,0:T(8,128)(2,1)S(1)}, bf16[3,128,640]{2,1,0:T(8,128)(2,1)}, u32[]{:S(2)}, u32[]{:S(2)}) %collective-permute-start.9) | collective-permute-done | bytes 491552 | tf_op jit(solution)/shard_map/ppermute | solution.py:48
  55.8 1.9 collective-permute-start.15
  62.7 11.3 %shard_map.180 = (f32[512,640]{1,0:T(8,128)S(1)}, bf16[512,640]{1,0:T(8,128)(2,1)S(1)}, bf16[512,640]{1,0:T(8,128)(2,1)S(1)}, bf16[4,512,256]{2,1,0:T(8,128)(2,1...) custom-call(s32[1]{0:T(128)} %bitcast.refs_0_, ...), custom_call_target="tpu_custom_call" | custom-call | flops 6000000000 | bytes 17485828 | tf_op jit(solution)/shard_map/pallas_call | solution.py:93
  78.4 3.6 %collective-permute-done.16.refs_3_ = bf16[6,128,640]{2,1,0:T(8,128)(2,1)} collective-permute-done((bf16[6,128,640]{2,1,0:T(8,128)(2,1)S(1)}, bf16[6,128,640]{2,1,0:T(8,128)(2,1)}, u32[]{:S(2)}, u32[]{:S(2)}) %collective-permute-start.16) | collective-permute-done | bytes 983072 | tf_op jit(solution)/shard_map/ppermute | solution.py:48
  83.1 10.2 %shard_map.182 = (f32[512,640]{1,0:T(8,128)S(1)}, f32[512,640]{1,0:T(8,128)S(1)}, bf16[4,6,128,640]{3,2,1,0:T(8,128)(2,1)S(1)}) custom-call(bf16[512,640]{1,0:T(8,128)(2,1)S(1)} %get-tuple-element.74.refs_4_.refs_0_, bf16[512,640]{1,0:T(8,128)(2,1)S(1)} %copy-done.12, f32[512,640]{1,0:T(8,128)S(1)} %get-tuple-element.75.refs_2_.refs_3_.refs_0_, ...), custom_call_target="tpu_custom_call" | custom-call | flops 6039797760 | bytes 14417920 | tf_op jit(solution)/shard_map/pallas_call | solution.py:93
  93.4 11.9 %shard_map.183 = (f32[512,640]{1,0:T(8,128)}, f32[512,640]{1,0:T(8,128)S(1)}, bf16[4,6,128,640]{3,2,1,0:T(8,128)(2,1)S(1)}, bf16[512,640]{1,0:T(8,128)(2,1)}) custom-call(bf16[512,640]{1,0:T(8,128)(2,1)S(1)} %get-tuple-element.74.refs_4_.refs_0_, bf16[512,640]{1,0:T(8,128)(2,1)S(1)} %copy-done.12, f32[512,640]{1,0:T(8,128)S(1)} %get-tuple-element.81.refs_2_, ...), custom_call_target="tpu_custom_call" | custom-call | flops 6039797760 | bytes 15073280 | tf_op jit(solution)/shard_map/pallas_call | solution.py:93
  107.2 8.1 %shard_map.184 = (f32[512,640]{1,0:T(8,128)S(1)}, bf16[512,640]{1,0:T(8,128)(2,1)S(1)}, bf16[512,1024]{1,0:T(8,128)(2,1)S(1)}, f32[512,512]{1,0:T(8,128)S(1)}, b...) custom-call(f32[512,640]{1,0:T(8,128)S(1)} %copy-done.22, f32[512,640]{1,0:T(8,128)S(1)} %get-tuple-element.85.refs_1_, ...), custom_call_target="tpu_custom_call" | custom-call | flops 5000000000 | bytes 13541376 | tf_op jit(solution)/shard_map/pallas_call | solution.py:93
  116.8 1.6 shard_map.185
  118.5 2.6 %shard_map.186 = (f32[512,640]{1,0:T(8,128)S(1)}, bf16[1024,640]{1,0:T(8,128)(2,1)S(1)}, bf16[1024,640]{1,0:T(8,128)(2,1)S(1)}) custom-call(bf16[512,640]{1,0:T(8,128)(2,1)S(1)} %get-tuple-element.84.refs_0_.refs_1_, bf16[512,640]{1,0:T(8,128)(2,1)S(1)} %get-tuple-element.94.refs_2_.refs_1_, bf16[512,1024]{1,0:T(8,128)(2,1)S(1)} %copy-done.18, ...), custom_call_target="tpu_custom_call" | custom-call | flops 2000000000 | bytes 8650752 | tf_op jit(solution)/shard_map/pallas_call | solution.py:93
  121.1 3.2 %shard_map.187 = (f32[512,640]{1,0:T(8,128)}, bf16[4,3,128,640]{3,2,1,0:T(8,128)(2,1)S(1)}, bf16[4,3,128,640]{3,2,1,0:T(8,128)(2,1)S(1)}) custom-call(bf16[512,640]{1,0:T(8,128)(2,1)S(1)} %copy-done.1, bf16[512,640]{1,0:T(8,128)(2,1)S(1)} %get-tuple-element.84.refs_0_.refs_1_, f32[512,512]{1,0:T(8,128)S(1)} %get-tuple-element.91.refs_2_, ...), custom_call_target="tpu_custom_call" | custom-call | flops 2000000000 | bytes 15278080 | tf_op jit(solution)/shard_map/pallas_call | solution.py:93
  124.3 5.1 %collective-permute-start.23 = (bf16[4,3,128,640]{3,2,1,0:T(8,128)(2,1)S(1)}, bf16[4,3,128,640]{3,2,1,0:T(8,128)(2,1)S(1)}, u32[]{:S(2)}, u32[]{:S(2)}) collective-permute-start(bf16[4,3,128,640]{3,2,1,0:T(8,128)(2,1)S(1)} %get-tuple-element.108), channel_id=1, source_target_pairs={{0,1},{1,0},{2,3},{3,2},{4,5},{5,4},{6,7},{7,6},{8,9},{9,8},{10,11... | collective-permute-start | bytes 5898248 | tf_op jit(solution)/shard_map/ppermute | solution.py:43
  129.9 3.7 %collective-permute-start.28 = (bf16[6,128,640]{2,1,0:T(8,128)(2,1)S(1)}, bf16[6,128,640]{2,1,0:T(8,128)(2,1)S(1)}, u32[]{:S(2)}, u32[]{:S(2)}) collective-permute-start(bf16[6,128,640]{2,1,0:T(8,128)(2,1)S(1)} %get-tuple-element.114), channel_id=1, source_target_pairs={{0,4},{1,17},{2,6},{3,19},{4,0},{5,21},{6,2},{7,23},{8,12},{9,25},... | collective-permute-start | bytes 2949128 | tf_op jit(solution)/shard_map/ppermute | solution.py:54
  134.5 1.8 collective-permute-start.24
  137.8 7.0 %collective-permute-done.27.refs_1_ = bf16[6,128,640]{2,1,0:T(8,128)(2,1)S(1)} collective-permute-done((bf16[6,128,640]{2,1,0:T(8,128)(2,1)S(1)}, bf16[6,128,640]{2,1,0:T(8,128)(2,1)S(1)}, u32[]{:S(2)}, u32[]{:S(2)}) %collective-permute-start.27) | collective-permute-done | bytes 983072 | tf_op jit(solution)/shard_map/ppermute | solution.py:54
  146.3 10.1 %collective-permute-done.28.refs_2_ = bf16[6,128,640]{2,1,0:T(8,128)(2,1)S(1)} collective-permute-done((bf16[6,128,640]{2,1,0:T(8,128)(2,1)S(1)}, bf16[6,128,640]{2,1,0:T(8,128)(2,1)S(1)}, u32[]{:S(2)}, u32[]{:S(2)}) %collective-permute-start.28) | collective-permute-done | bytes 983072 | tf_op jit(solution)/shard_map/ppermute | solution.py:54
  157.1 4.0 %collective-permute-start.34 = (bf16[6,32,640]{2,1,0:T(8,128)(2,1)S(1)}, bf16[6,32,640]{2,1,0:T(8,128)(2,1)S(1)}, u32[]{:S(2)}, u32[]{:S(2)}) collective-permute-start(bf16[6,32,640]{2,1,0:T(8,128)(2,1)S(1)} %get-tuple-element.122), channel_id=1, source_target_pairs={{0,16},{1,5},{2,18},{3,7},{4,20},{5,1},{6,22},{7,3},{8,24},{9,13},... | collective-permute-start | bytes 737288 | tf_op jit(solution)/shard_map/ppermute | solution.py:54
  161.5 1.8 collective-permute-start.35
  163.3 8.8 %collective-permute-done.25.refs_2_ = bf16[3,128,640]{2,1,0:T(8,128)(2,1)S(1)} collective-permute-done((bf16[3,128,640]{2,1,0:T(8,128)(2,1)S(1)}, bf16[3,128,640]{2,1,0:T(8,128)(2,1)S(1)}, u32[]{:S(2)}, u32[]{:S(2)}) %collective-permute-start.25) | collective-permute-done | bytes 491552 | tf_op jit(solution)/shard_map/ppermute | solution.py:54
  172.6 4.0 %collective-permute-start.31 = (bf16[3,32,640]{2,1,0:T(8,128)(2,1)S(1)}, bf16[3,32,640]{2,1,0:T(8,128)(2,1)S(1)}, u32[]{:S(2)}, u32[]{:S(2)}) collective-permute-start(bf16[3,32,640]{2,1,0:T(8,128)(2,1)S(1)} %get-tuple-element.119), channel_id=1, source_target_pairs={{0,16},{1,5},{2,18},{3,7},{4,20},{5,1},{6,22},{7,3},{8,24},{9,13},... | collective-permute-start | bytes 368648 | tf_op jit(solution)/shard_map/ppermute | solution.py:54
  176.7 1.8 collective-permute-done.30.refs_1_
  178.5 2.3 %collective-permute-done.31.refs_2_ = bf16[3,32,640]{2,1,0:T(8,128)(2,1)S(1)} collective-permute-done((bf16[3,32,640]{2,1,0:T(8,128)(2,1)S(1)}, bf16[3,32,640]{2,1,0:T(8,128)(2,1)S(1)}, u32[]{:S(2)}, u32[]{:S(2)}) %collective-permute-start.31) | collective-permute-done | bytes 122912 | tf_op jit(solution)/shard_map/ppermute | solution.py:54
  183.2 2.5 %collective-permute-start.38 = (bf16[9,8,640]{2,1,0:T(8,128)(2,1)S(1)}, bf16[9,8,640]{2,1,0:T(8,128)(2,1)S(1)}, u32[]{:S(2)}, u32[]{:S(2)}) collective-permute-start(bf16[9,8,640]{2,1,0:T(8,128)(2,1)S(1)} %get-tuple-element.127), channel_id=1, source_target_pairs={{0,96},{1,97},{2,98},{3,99},{4,100},{5,101},{6,102},{7,103},{8,104... | collective-permute-start | bytes 276488 | tf_op jit(solution)/shard_map/ppermute | solution.py:54
  185.7 2.7 %collective-permute-done.36.refs_2_ = bf16[9,8,640]{2,1,0:T(8,128)(2,1)S(1)} collective-permute-done((bf16[9,8,640]{2,1,0:T(8,128)(2,1)S(1)}, bf16[9,8,640]{2,1,0:T(8,128)(2,1)S(1)}, u32[]{:S(2)}, u32[]{:S(2)}) %collective-permute-start.36) | collective-permute-done | bytes 92192 | tf_op jit(solution)/shard_map/ppermute | solution.py:54
  (129 shorter events, 38.5 us)
Async XLA Ops:
  0.6 35.6 %collective-permute-start = (bf16[512,640]{1,0:T(8,128)(2,1)}, bf16[512,640]{1,0:T(8,128)(2,1)S(1)}, u32[]{:S(2)}, u32[]{:S(2)}) collective-permute-start(bf16[512,640]{1,0:T(8,128)(2,1)} %refs_0_.1), channel_id=1, source_target_pairs={{0,1},{1,2},{2,3},{3,4},{4,5},{5,6},{6,7},{7,8},{8,9},{9,10},{10,1... | collective-permute-start | bytes 1966088 | tf_op jit(solution)/shard_map/ppermute | solution.py:62
  12.0 8.2 %collective-permute-start.3 = (bf16[9,8,640]{2,1,0:T(8,128)(2,1)S(1)}, bf16[9,8,640]{2,1,0:T(8,128)(2,1)S(1)}, u32[]{:S(2)}, u32[]{:S(2)}) collective-permute-start(bf16[9,8,640]{2,1,0:T(8,128)(2,1)S(1)} %shard_map.177.refs_0_), channel_id=1, source_target_pairs={{0,32},{1,33},{2,34},{3,35},{4,36},{5,37},{6,38},{7,39},{8,40},{9,... | collective-permute-start | bytes 276488 | tf_op jit(solution)/shard_map/ppermute | solution.py:48
  20.2 12.1 %collective-permute-start.4 = (bf16[9,4,8,640]{3,2,1,0:T(8,128)(2,1)S(1)}, bf16[9,4,8,640]{3,2,1,0:T(8,128)(2,1)S(1)}, u32[]{:S(2)}, u32[]{:S(2)}) collective-permute-start(bf16[9,4,8,640]{3,2,1,0:T(8,128)(2,1)S(1)} %shard_map.178.refs_0_), channel_id=1, source_target_pairs={{0,24},{1,7},{2,26},{3,1},{4,28},{5,3},{6,30},{7,5},{8,0},{9,15},{... | collective-permute-start | bytes 1105928 | tf_op jit(solution)/shard_map/ppermute | solution.py:48
  23.3 9.1 %collective-permute-start.5 = (bf16[9,4,8,640]{3,2,1,0:T(8,128)(2,1)S(1)}, bf16[9,4,8,640]{3,2,1,0:T(8,128)(2,1)S(1)}, u32[]{:S(2)}, u32[]{:S(2)}) collective-permute-start(bf16[9,4,8,640]{3,2,1,0:T(8,128)(2,1)S(1)} %shard_map.178.refs_0_), channel_id=1, source_target_pairs={{0,16},{1,5},{2,18},{3,7},{4,20},{5,1},{6,22},{7,3},{8,24},{9,13},... | collective-permute-start | bytes 1105928 | tf_op jit(solution)/shard_map/ppermute | solution.py:48
  23.9 12.3 %collective-permute-start.6 = (bf16[9,4,8,640]{3,2,1,0:T(8,128)(2,1)S(1)}, bf16[9,4,8,640]{3,2,1,0:T(8,128)(2,1)S(1)}, u32[]{:S(2)}, u32[]{:S(2)}) collective-permute-start(bf16[9,4,8,640]{3,2,1,0:T(8,128)(2,1)S(1)} %shard_map.178.refs_0_), channel_id=1, source_target_pairs={{0,8},{1,3},{2,10},{3,5},{4,12},{5,7},{6,14},{7,1},{8,16},{9,11},{... | collective-permute-start | bytes 1105928 | tf_op jit(solution)/shard_map/ppermute | solution.py:48
  36.4 13.8 %collective-permute-start.7 = (bf16[3,128,640]{2,1,0:T(8,128)(2,1)S(1)}, bf16[3,128,640]{2,1,0:T(8,128)(2,1)}, u32[]{:S(2)}, u32[]{:S(2)}) collective-permute-start(bf16[3,128,640]{2,1,0:T(8,128)(2,1)S(1)} %bitcast.11), channel_id=1, source_target_pairs={{0,6},{1,25},{2,0},{3,27},{4,2},{5,29},{6,4},{7,31},{8,14},{9,1},{... | collective-permute-start | bytes 1474568 | tf_op jit(solution)/shard_map/ppermute | solution.py:48
  38.6 11.7 %collective-permute-start.8 = (bf16[3,128,640]{2,1,0:T(8,128)(2,1)S(1)}, bf16[3,128,640]{2,1,0:T(8,128)(2,1)}, u32[]{:S(2)}, u32[]{:S(2)}) collective-permute-start(bf16[3,128,640]{2,1,0:T(8,128)(2,1)S(1)} %bitcast.12), channel_id=1, source_target_pairs={{0,4},{1,17},{2,6},{3,19},{4,0},{5,21},{6,2},{7,23},{8,12},{9,25},... | collective-permute-start | bytes 1474568 | tf_op jit(solution)/shard_map/ppermute | solution.py:48
  40.5 13.8 %collective-permute-start.9 = (bf16[3,128,640]{2,1,0:T(8,128)(2,1)S(1)}, bf16[3,128,640]{2,1,0:T(8,128)(2,1)}, u32[]{:S(2)}, u32[]{:S(2)}) collective-permute-start(bf16[3,128,640]{2,1,0:T(8,128)(2,1)S(1)} %bitcast.13), channel_id=1, source_target_pairs={{0,2},{1,9},{2,4},{3,11},{4,6},{5,13},{6,0},{7,15},{8,10},{9,17},{... | collective-permute-start | bytes 1474568 | tf_op jit(solution)/shard_map/ppermute | solution.py:48
  41.8 13.2 %collective-permute-start.10 = (bf16[3,128,640]{2,1,0:T(8,128)(2,1)S(1)}, bf16[3,128,640]{2,1,0:T(8,128)(2,1)S(1)}, u32[]{:S(2)}, u32[]{:S(2)}) collective-permute-start(bf16[3,128,640]{2,1,0:T(8,128)(2,1)S(1)} %bitcast.14), channel_id=1, source_target_pairs={{0,1},{1,0},{2,3},{3,2},{4,5},{5,4},{6,7},{7,6},{8,9},{9,8},{10,11... | collective-permute-start | bytes 1474568 | tf_op jit(solution)/shard_map/ppermute | solution.py:43
  50.2 7.4 %collective-permute-start.11 = (bf16[3,128,640]{2,1,0:T(8,128)(2,1)}, bf16[3,128,640]{2,1,0:T(8,128)(2,1)}, u32[]{:S(2)}, u32[]{:S(2)}) collective-permute-start(bf16[3,128,640]{2,1,0:T(8,128)(2,1)} %collective-permute-done.7.refs_5_), channel_id=1, source_target_pairs={{0,1},{1,0},{2,3},{3,2},{4,5},{5,4},{6,7},{7,6},{8,9},{9,8},{10,11... | collective-permute-start | bytes 1474568 | tf_op jit(solution)/shard_map/ppermute | solution.py:43
  50.3 9.2 %collective-permute-start.12 = (bf16[3,128,640]{2,1,0:T(8,128)(2,1)}, bf16[3,128,640]{2,1,0:T(8,128)(2,1)}, u32[]{:S(2)}, u32[]{:S(2)}) collective-permute-start(bf16[3,128,640]{2,1,0:T(8,128)(2,1)} %collective-permute-done.8.refs_6_), channel_id=1, source_target_pairs={{0,1},{1,0},{2,3},{3,2},{4,5},{5,4},{6,7},{7,6},{8,9},{9,8},{10,11... | collective-permute-start | bytes 1474568 | tf_op jit(solution)/shard_map/ppermute | solution.py:43
  54.3 24.0 %collective-permute-start.14 = (bf16[6,128,640]{2,1,0:T(8,128)(2,1)S(1)}, bf16[6,128,640]{2,1,0:T(8,128)(2,1)S(1)}, u32[]{:S(2)}, u32[]{:S(2)}) collective-permute-start(bf16[6,128,640]{2,1,0:T(8,128)(2,1)S(1)} %bitcast.5), channel_id=1, source_target_pairs={{0,6},{1,25},{2,0},{3,27},{4,2},{5,29},{6,4},{7,31},{8,14},{9,1},{... | collective-permute-start | bytes 2949128 | tf_op jit(solution)/shard_map/ppermute | solution.py:48
  55.8 22.6 %collective-permute-start.15 = (bf16[6,128,640]{2,1,0:T(8,128)(2,1)S(1)}, bf16[6,128,640]{2,1,0:T(8,128)(2,1)S(1)}, u32[]{:S(2)}, u32[]{:S(2)}) collective-permute-start(bf16[6,128,640]{2,1,0:T(8,128)(2,1)S(1)} %bitcast.6), channel_id=1, source_target_pairs={{0,4},{1,17},{2,6},{3,19},{4,0},{5,21},{6,2},{7,23},{8,12},{9,25},... | collective-permute-start | bytes 2949128 | tf_op jit(solution)/shard_map/ppermute | solution.py:48
  57.6 24.3 %collective-permute-start.16 = (bf16[6,128,640]{2,1,0:T(8,128)(2,1)S(1)}, bf16[6,128,640]{2,1,0:T(8,128)(2,1)}, u32[]{:S(2)}, u32[]{:S(2)}) collective-permute-start(bf16[6,128,640]{2,1,0:T(8,128)(2,1)S(1)} %bitcast.7), channel_id=1, source_target_pairs={{0,2},{1,9},{2,4},{3,11},{4,6},{5,13},{6,0},{7,15},{8,10},{9,17},{... | collective-permute-start | bytes 2949128 | tf_op jit(solution)/shard_map/ppermute | solution.py:48
  82.0 11.3 %collective-permute-start.17 = (bf16[6,128,640]{2,1,0:T(8,128)(2,1)S(1)}, bf16[6,128,640]{2,1,0:T(8,128)(2,1)S(1)}, u32[]{:S(2)}, u32[]{:S(2)}) collective-permute-start(bf16[6,128,640]{2,1,0:T(8,128)(2,1)S(1)} %get-tuple-element.77.refs_4_), channel_id=1, source_target_pairs={{0,1},{1,0},{2,3},{3,2},{4,5},{5,4},{6,7},{7,6},{8,9},{9,8},{10,11... | collective-permute-start | bytes 2949128 | tf_op jit(solution)/shard_map/ppermute | solution.py:43
  82.1 11.2 %collective-permute-start.18 = (bf16[6,128,640]{2,1,0:T(8,128)(2,1)S(1)}, bf16[6,128,640]{2,1,0:T(8,128)(2,1)S(1)}, u32[]{:S(2)}, u32[]{:S(2)}) collective-permute-start(bf16[6,128,640]{2,1,0:T(8,128)(2,1)S(1)} %get-tuple-element.78.refs_5_), channel_id=1, source_target_pairs={{0,1},{1,0},{2,3},{3,2},{4,5},{5,4},{6,7},{7,6},{8,9},{9,8},{10,11... | collective-permute-start | bytes 2949128 | tf_op jit(solution)/shard_map/ppermute | solution.py:43
  82.6 10.7 %collective-permute-start.19 = (bf16[6,128,640]{2,1,0:T(8,128)(2,1)S(1)}, bf16[6,128,640]{2,1,0:T(8,128)(2,1)S(1)}, u32[]{:S(2)}, u32[]{:S(2)}) collective-permute-start(bf16[6,128,640]{2,1,0:T(8,128)(2,1)S(1)} %get-tuple-element.79.refs_6_), channel_id=1, source_target_pairs={{0,1},{1,0},{2,3},{3,2},{4,5},{5,4},{6,7},{7,6},{8,9},{9,8},{10,11... | collective-permute-start | bytes 2949128 | tf_op jit(solution)/shard_map/ppermute | solution.py:43
  82.7 10.6 %collective-permute-start.20 = (bf16[6,128,640]{2,1,0:T(8,128)(2,1)}, bf16[6,128,640]{2,1,0:T(8,128)(2,1)S(1)}, u32[]{:S(2)}, u32[]{:S(2)}) collective-permute-start(bf16[6,128,640]{2,1,0:T(8,128)(2,1)} %get-tuple-element.80.refs_7_), channel_id=1, source_target_pairs={{0,1},{1,0},{2,3},{3,2},{4,5},{5,4},{6,7},{7,6},{8,9},{9,8},{10,11... | collective-permute-start | bytes 2949128 | tf_op jit(solution)/shard_map/ppermute | solution.py:43
  105.2 11.5 %collective-permute-start.22 = (bf16[4,6,128,640]{3,2,1,0:T(8,128)(2,1)S(1)}, bf16[4,6,128,640]{3,2,1,0:T(8,128)(2,1)S(1)}, u32[]{:S(2)}, u32[]{:S(2)}) collective-permute-start(bf16[4,6,128,640]{3,2,1,0:T(8,128)(2,1)S(1)} %get-tuple-element.99), channel_id=1, source_target_pairs={{0,1},{1,0},{2,3},{3,2},{4,5},{5,4},{6,7},{7,6},{8,9},{9,8},{10,11... | collective-permute-start | bytes 11796488 | tf_op jit(solution)/shard_map/ppermute | solution.py:43
  124.3 9.7 %collective-permute-start.23 = (bf16[4,3,128,640]{3,2,1,0:T(8,128)(2,1)S(1)}, bf16[4,3,128,640]{3,2,1,0:T(8,128)(2,1)S(1)}, u32[]{:S(2)}, u32[]{:S(2)}) collective-permute-start(bf16[4,3,128,640]{3,2,1,0:T(8,128)(2,1)S(1)} %get-tuple-element.108), channel_id=1, source_target_pairs={{0,1},{1,0},{2,3},{3,2},{4,5},{5,4},{6,7},{7,6},{8,9},{9,8},{10,11... | collective-permute-start | bytes 5898248 | tf_op jit(solution)/shard_map/ppermute | solution.py:43
  129.4 15.3 %collective-permute-start.27 = (bf16[6,128,640]{2,1,0:T(8,128)(2,1)S(1)}, bf16[6,128,640]{2,1,0:T(8,128)(2,1)S(1)}, u32[]{:S(2)}, u32[]{:S(2)}) collective-permute-start(bf16[6,128,640]{2,1,0:T(8,128)(2,1)S(1)} %get-tuple-element.100.refs_5_), channel_id=1, source_target_pairs={{0,2},{1,9},{2,4},{3,11},{4,6},{5,13},{6,0},{7,15},{8,10},{9,17},{... | collective-permute-start | bytes 2949128 | tf_op jit(solution)/shard_map/ppermute | solution.py:54
  129.9 26.5 %collective-permute-start.28 = (bf16[6,128,640]{2,1,0:T(8,128)(2,1)S(1)}, bf16[6,128,640]{2,1,0:T(8,128)(2,1)S(1)}, u32[]{:S(2)}, u32[]{:S(2)}) collective-permute-start(bf16[6,128,640]{2,1,0:T(8,128)(2,1)S(1)} %get-tuple-element.114), channel_id=1, source_target_pairs={{0,4},{1,17},{2,6},{3,19},{4,0},{5,21},{6,2},{7,23},{8,12},{9,25},... | collective-permute-start | bytes 2949128 | tf_op jit(solution)/shard_map/ppermute | solution.py:54
  133.6 22.7 %collective-permute-start.29 = (bf16[6,128,640]{2,1,0:T(8,128)(2,1)S(1)}, bf16[6,128,640]{2,1,0:T(8,128)(2,1)S(1)}, u32[]{:S(2)}, u32[]{:S(2)}) collective-permute-start(bf16[6,128,640]{2,1,0:T(8,128)(2,1)S(1)} %get-tuple-element.115), channel_id=1, source_target_pairs={{0,6},{1,25},{2,0},{3,27},{4,2},{5,29},{6,4},{7,31},{8,14},{9,1},{... | collective-permute-start | bytes 2949128 | tf_op jit(solution)/shard_map/ppermute | solution.py:54
  134.5 27.0 %collective-permute-start.24 = (bf16[3,128,640]{2,1,0:T(8,128)(2,1)S(1)}, bf16[3,128,640]{2,1,0:T(8,128)(2,1)S(1)}, u32[]{:S(2)}, u32[]{:S(2)}) collective-permute-start(bf16[3,128,640]{2,1,0:T(8,128)(2,1)S(1)} %get-tuple-element.110.refs_4_), channel_id=1, source_target_pairs={{0,2},{1,9},{2,4},{3,11},{4,6},{5,13},{6,0},{7,15},{8,10},{9,17},{... | collective-permute-start | bytes 1474568 | tf_op jit(solution)/shard_map/ppermute | solution.py:54
  136.2 35.9 %collective-permute-start.25 = (bf16[3,128,640]{2,1,0:T(8,128)(2,1)S(1)}, bf16[3,128,640]{2,1,0:T(8,128)(2,1)S(1)}, u32[]{:S(2)}, u32[]{:S(2)}) collective-permute-start(bf16[3,128,640]{2,1,0:T(8,128)(2,1)S(1)} %get-tuple-element.111), channel_id=1, source_target_pairs={{0,4},{1,17},{2,6},{3,19},{4,0},{5,21},{6,2},{7,23},{8,12},{9,25},... | collective-permute-start | bytes 1474568 | tf_op jit(solution)/shard_map/ppermute | solution.py:54
  144.8 27.3 %collective-permute-start.26 = (bf16[3,128,640]{2,1,0:T(8,128)(2,1)S(1)}, bf16[3,128,640]{2,1,0:T(8,128)(2,1)S(1)}, u32[]{:S(2)}, u32[]{:S(2)}) collective-permute-start(bf16[3,128,640]{2,1,0:T(8,128)(2,1)S(1)} %get-tuple-element.112), channel_id=1, source_target_pairs={{0,6},{1,25},{2,0},{3,27},{4,2},{5,29},{6,4},{7,31},{8,14},{9,1},{... | collective-permute-start | bytes 1474568 | tf_op jit(solution)/shard_map/ppermute | solution.py:54
  156.9 19.7 %collective-permute-start.33 = (bf16[6,32,640]{2,1,0:T(8,128)(2,1)S(1)}, bf16[6,32,640]{2,1,0:T(8,128)(2,1)S(1)}, u32[]{:S(2)}, u32[]{:S(2)}) collective-permute-start(bf16[6,32,640]{2,1,0:T(8,128)(2,1)S(1)} %get-tuple-element.116.refs_4_), channel_id=1, source_target_pairs={{0,8},{1,3},{2,10},{3,5},{4,12},{5,7},{6,14},{7,1},{8,16},{9,11},{... | collective-permute-start | bytes 737288 | tf_op jit(solution)/shard_map/ppermute | solution.py:54
  157.1 19.5 %collective-permute-start.34 = (bf16[6,32,640]{2,1,0:T(8,128)(2,1)S(1)}, bf16[6,32,640]{2,1,0:T(8,128)(2,1)S(1)}, u32[]{:S(2)}, u32[]{:S(2)}) collective-permute-start(bf16[6,32,640]{2,1,0:T(8,128)(2,1)S(1)} %get-tuple-element.122), channel_id=1, source_target_pairs={{0,16},{1,5},{2,18},{3,7},{4,20},{5,1},{6,22},{7,3},{8,24},{9,13},... | collective-permute-start | bytes 737288 | tf_op jit(solution)/shard_map/ppermute | solution.py:54
  161.5 15.2 %collective-permute-start.35 = (bf16[6,32,640]{2,1,0:T(8,128)(2,1)S(1)}, bf16[6,32,640]{2,1,0:T(8,128)(2,1)S(1)}, u32[]{:S(2)}, u32[]{:S(2)}) collective-permute-start(bf16[6,32,640]{2,1,0:T(8,128)(2,1)S(1)} %get-tuple-element.123), channel_id=1, source_target_pairs={{0,24},{1,7},{2,26},{3,1},{4,28},{5,3},{6,30},{7,5},{8,0},{9,15},{... | collective-permute-start | bytes 737288 | tf_op jit(solution)/shard_map/ppermute | solution.py:54
  172.6 8.1 %collective-permute-start.31 = (bf16[3,32,640]{2,1,0:T(8,128)(2,1)S(1)}, bf16[3,32,640]{2,1,0:T(8,128)(2,1)S(1)}, u32[]{:S(2)}, u32[]{:S(2)}) collective-permute-start(bf16[3,32,640]{2,1,0:T(8,128)(2,1)S(1)} %get-tuple-element.119), channel_id=1, source_target_pairs={{0,16},{1,5},{2,18},{3,7},{4,20},{5,1},{6,22},{7,3},{8,24},{9,13},... | collective-permute-start | bytes 368648 | tf_op jit(solution)/shard_map/ppermute | solution.py:54
  181.6 6.8 %collective-permute-start.36 = (bf16[9,8,640]{2,1,0:T(8,128)(2,1)S(1)}, bf16[9,8,640]{2,1,0:T(8,128)(2,1)S(1)}, u32[]{:S(2)}, u32[]{:S(2)}) collective-permute-start(bf16[9,8,640]{2,1,0:T(8,128)(2,1)S(1)} %get-tuple-element.125), channel_id=1, source_target_pairs={{0,32},{1,33},{2,34},{3,35},{4,36},{5,37},{6,38},{7,39},{8,40},{9,... | collective-permute-start | bytes 276488 | tf_op jit(solution)/shard_map/ppermute | solution.py:54
  181.7 6.7 %collective-permute-start.37 = (bf16[9,8,640]{2,1,0:T(8,128)(2,1)S(1)}, bf16[9,8,640]{2,1,0:T(8,128)(2,1)S(1)}, u32[]{:S(2)}, u32[]{:S(2)}) collective-permute-start(bf16[9,8,640]{2,1,0:T(8,128)(2,1)S(1)} %get-tuple-element.126), channel_id=1, source_target_pairs={{0,64},{1,65},{2,66},{3,67},{4,68},{5,69},{6,70},{7,71},{8,72},{9,... | collective-permute-start | bytes 276488 | tf_op jit(solution)/shard_map/ppermute | solution.py:54
  (36 other events, 141.6 us)
